TPU v7x, 768 devices: a whole 4x8x12 slice. The times are simulated.
768 devices in a mesh: slab: 96 (over z, y_hi, core), grp: 8 (over x, y_lo).
Axes of the slice: x: 4, y: 8 (y_hi: 4, y_lo: 2; y = y_hi * 2 + y_lo), z: 12, core: 2. Of those that a mesh axis runs over, the one named last changes fastest.
Arguments:
- positions: float32 [3, 49152], P(None, ('slab', 'grp')), may hold values from 0 to 2
- species: int32 [49152], P(('slab', 'grp')), may hold values from 0 to 3
- node_state: bfloat16 [49152, 128], P(('slab', 'grp')), may hold values from -6 to 6
- w_self: bfloat16 [128, 128], replicated, may hold values from -0.5 to 0.5
- w_send: bfloat16 [128, 128], replicated, may hold values from -0.5 to 0.5
- radial: float32 [8, 128], replicated, may hold values from -2 to 2
- w_mix: bfloat16 [128, 128], replicated, may hold values from -0.5 to 0.5
- readout: float32 [128], replicated, may hold values from -0.078125 to 0.078125
- pair_scale: float32 [4, 4], replicated, may hold values from 0.5 to 2
- nbr_blocks: int32 [768, 4], P(('slab', 'grp')), may hold values from 0 to 23, as said below
- tile_count: int32 [768], P(('slab', 'grp')), may hold values from 2 to 4
Outputs:
- atom_energy: float32 [49152], P(('slab', 'grp'))
- forces: float32 [3, 49152], P(None, ('slab', 'grp'))
Inputs may be any that keep to these rules, and one draw needn't show every extreme that they name: `nbr_blocks`: in every row, entry 0 is below 8 (a block of the lower slab's group) and entry 1 is at least 2 * 8 (a block of the upper slab's group).
All inputs are finite; a program needn't handle non-finite values.
Results may differ from a plain program's by a relative error of at most 0.0022.
Values sent between devices are 32-bit elements; how exact they have to be, the bound alone decides.
A program may use at most 32 MiB of HBM per device.

v0:
```python
import jax
import jax.numpy as jnp
from jax import lax
from jax.sharding import PartitionSpec as P

BLOCK = 64


def with_halo(block, sides, width):
    for axis, dim in sides:
        count = lax.axis_size(axis)
        forward = [(i, i + 1) for i in range(count - 1)]
        forward.append((count - 1, 0))
        backward = [(target, source) for source, target in forward]
        low = lax.ppermute(
            lax.slice_in_dim(block, block.shape[dim] - width, None, axis=dim), axis, forward
        )
        high = lax.ppermute(lax.slice_in_dim(block, 0, width, axis=dim), axis, backward)
        block = jnp.concatenate([low, block, high], axis=dim)
    return block


def from_behind(value, axis, steps):
    count = lax.axis_size(axis)
    pairs = [(source, (source + steps) % count) for source in range(count)]
    return lax.ppermute(value, axis, pairs)


def pair_tile(pos_i, pos_j, spc_i, spc_j, self_i, send_j, keep, radial, w_mix, readout, pair_scale):
    diff = pos_j[:, None, :] - pos_i[:, :, None]
    dist_sq = jnp.sum(diff * diff, axis=0)
    kinds = jnp.arange(pair_scale.shape[0]).astype(jnp.float32)
    onehot_i = (spc_i[:, None] == kinds[None, :]).astype(jnp.float32)
    onehot_j = (spc_j[:, None] == kinds[None, :]).astype(jnp.float32)
    scale = jnp.dot(
        jnp.dot(onehot_i, pair_scale, precision=lax.Precision.HIGHEST),
        onehot_j.T,
        precision=lax.Precision.HIGHEST,
    )
    scaled = dist_sq * scale
    cutoff = jnp.maximum(1.0 - scaled / 2.5, 0.0) ** 2
    nbasis = radial.shape[0]
    spacing = 2.5 / (nbasis - 1)
    centers = jnp.arange(nbasis).astype(jnp.float32) * spacing
    basis = jnp.exp(-(((scaled[:, :, None] - centers) / spacing) ** 2))
    atom_block_list = pos_i.shape[1]
    width = radial.shape[1]
    latent = (
        self_i[:, None, :]
        + send_j[None, :, :]
        + jnp.einsum("ijm,mc->ijc", basis, radial, precision=lax.Precision.HIGHEST)
    )
    hidden = (
        jax.nn.silu(latent).astype(jnp.bfloat16).reshape(atom_block_list * atom_block_list, width)
    )
    mixed = jax.nn.silu(jnp.dot(hidden, w_mix, preferred_element_type=jnp.float32))
    energy = jnp.dot(mixed, readout, precision=lax.Precision.HIGHEST).reshape(
        atom_block_list, atom_block_list
    )
    return energy * cutoff * keep


def tile_grads(
    pos_i, pos_j, spc_i, spc_j, self_i, send_j, keep, radial, w_mix, readout, pair_scale
):

    def total(first, second):
        return pair_tile(
            first, second, spc_i, spc_j, self_i, send_j, keep, radial, w_mix, readout, pair_scale
        )

    pair, pullback = jax.vjp(total, pos_i, pos_j)
    grad_i, grad_j = pullback(jnp.ones_like(pair))
    return (jnp.sum(pair, axis=1), grad_i, grad_j)


def per_device(
    positions,
    species,
    node_state,
    w_self,
    w_send,
    radial,
    w_mix,
    readout,
    pair_scale,
    nbr_blocks,
    tile_count,
):
    block_groupings = lax.axis_size("grp")
    member = lax.axis_index("grp")
    atoms = positions.shape[1]
    nblk = nbr_blocks.shape[0]
    tiles = nbr_blocks.shape[1]
    self_feat = jnp.dot(node_state, w_self, preferred_element_type=jnp.float32)
    sender_features = jnp.dot(node_state, w_send, preferred_element_type=jnp.float32)
    species_labels = species.astype(jnp.float32)
    loop_carry_state = jnp.concatenate(
        [positions, species_labels[None, :], sender_features.T], axis=0
    )
    block_strip = lax.all_gather(loop_carry_state, "grp", axis=1, tiled=True)
    window = with_halo(block_strip, (("slab", 1),), block_groupings * atoms)
    span = window.shape[1]
    win_pos = window[0:3]
    win_spc = window[3]
    win_send = window[4:]
    own_base = block_groupings * nblk + member * nblk
    ident = jnp.eye(BLOCK, dtype=jnp.float32)

    def step(turn, carry):
        energy, own_grad, win_grad = carry
        block = turn // tiles
        slot = turn % tiles
        other = nbr_blocks[block, slot]
        start_j = other * BLOCK
        pos_j = lax.dynamic_slice_in_dim(win_pos, start_j, BLOCK, 1)
        spc_j = lax.dynamic_slice_in_dim(win_spc, start_j, BLOCK, 0)
        send_j = lax.dynamic_slice_in_dim(win_send, start_j, BLOCK, 1).T
        keep = jnp.where(other == own_base + block, 1.0 - ident, jnp.ones_like(ident))

        def active(ignored_argument):
            return tile_grads(
                positions,
                pos_j,
                species_labels,
                spc_j,
                self_feat,
                send_j,
                keep,
                radial,
                w_mix,
                readout,
                pair_scale,
            )

        def silent(ignored_argument):
            return (
                jnp.zeros((BLOCK,), jnp.float32),
                jnp.zeros((3, BLOCK), jnp.float32),
                jnp.zeros((3, BLOCK), jnp.float32),
            )

        part, grad_i, grad_j = lax.cond(slot < tile_count[block], active, silent, None)
        energy = energy + part
        own_grad = own_grad + grad_i
        win_grad = lax.dynamic_update_slice_in_dim(
            win_grad, lax.dynamic_slice_in_dim(win_grad, start_j, BLOCK, 1) + grad_j, start_j, 1
        )
        return (energy, own_grad, win_grad)

    start = (
        jnp.zeros((atoms,), jnp.float32),
        jnp.zeros((3, atoms), jnp.float32),
        jnp.zeros((3, span), jnp.float32),
    )
    energy, own_grad, win_grad = lax.fori_loop(0, nblk * tiles, step, start)
    third = block_groupings * atoms
    lower = win_grad[:, 0:third]
    central_block = win_grad[:, third : 2 * third]
    upper = win_grad[:, 2 * third :]
    panel_grad = central_block + from_behind(upper, "slab", 1) + from_behind(lower, "slab", -1)
    returned = lax.psum_scatter(panel_grad, "grp", scatter_dimension=1, tiled=True)
    forces = -(own_grad + returned)
    return (energy, forces)


def solution(mesh):
    return jax.shard_map(
        per_device,
        mesh=mesh,
        in_specs=(
            P(None, ("slab", "grp")),
            P(("slab", "grp")),
            P(("slab", "grp"), None),
            P(),
            P(),
            P(),
            P(),
            P(),
            P(),
            P(("slab", "grp"), None),
            P(("slab", "grp")),
        ),
        out_specs=(P(("slab", "grp")), P(None, ("slab", "grp"))),
        check_vma=False,
    )
```

profile of v0, /device:TPU:16, one launch (start us, length us, event | category | flops | bytes accessed | tf_op | source)
XLA Modules:
  0.0 208.9 jit_solution(887416516655256370)
XLA Ops:
  8.8 0.8 fusion.68
  9.7 30.0 %all_gather.3 = f32[132,512]{0,1:T(8,128)S(1)} all-gather(f32[132,64]{0,1:T(8,128)S(1)} %pad_maximum_fusion), channel_id=1, replica_groups=mesh['slab'=96,'grp'=8] {'grp'}, dimensions={1}, use_global_device_ids=true | all-gather | bytes 304128 | tf_op jit(solution)/shard_map/all_gather | solution.py:101
  39.8 1.9 collective-permute-start
  41.7 4.5 %collective-permute-start.1 = (f32[132,512]{0,1:T(8,128)S(1)}, f32[132,512]{0,1:T(8,128)S(1)}, u32[]{:S(2)}, u32[]{:S(2)}) collective-permute-start(f32[132,512]{0,1:T(8,128)S(1)} %all_gather.3), channel_id=1, source_target_pairs={{8,0},{16,8},{24,16},{32,24},{40,32},{48,40},{56,48},{64,56},{72,6... | collective-permute-start | bytes 811016 | tf_op jit(solution)/shard_map/ppermute | solution.py:18
  46.2 0.9 fusion.67
  47.1 4.1 %collective-permute-done = f32[132,512]{0,1:T(8,128)S(1)} collective-permute-done((f32[132,512]{0,1:T(8,128)S(1)}, f32[132,512]{0,1:T(8,128)S(1)}, u32[]{:S(2)}, u32[]{:S(2)}) %collective-permute-start) | collective-permute-done | bytes 270368 | tf_op jit(solution)/shard_map/ppermute | solution.py:15
  51.3 10.2 %collective-permute-done.1 = f32[132,512]{0,1:T(8,128)S(1)} collective-permute-done((f32[132,512]{0,1:T(8,128)S(1)}, f32[132,512]{0,1:T(8,128)S(1)}, u32[]{:S(2)}, u32[]{:S(2)}) %collective-permute-start.1) | collective-permute-done | bytes 270368 | tf_op jit(solution)/shard_map/ppermute | solution.py:18
  62.9 43.5 %while.20 = (s32[]{:T(128)}, f32[64]{0:T(128)S(1)}, f32[3,64]{1,0:T(4,128)S(1)}, f32[3,1536]{1,0:T(4,128)S(1)}, s32[1]{0:T(128)}, /*index=5*/s32[1,4]{1,0:T(1,12...) while((s32[]{:T(128)}, f32[64]{0:T(128)S(1)}, ...), condition=%wide.region_8.9_spmd.clone, body=%wide.region_0.8_spmd.clone.sunk | while | flops 394101760 | bytes 23932268 | solution.py:156
  64.9 17.1 %conditional.3 = (f32[64]{0:T(128)S(1)}, f32[3,64]{1,0:T(4,128)S(1)}, f32[3,64]{1,0:T(4,128)S(1)}) conditional(s32[]{:T(128)} %convert_element_type.79, () %tuple.95, (f32[64,128]{1,0:T(8,128)S(1)}, f32[64,128]{1,0:T(8,128)S(1)}, f32[3,1536]{1,0:T(4,128)S(1)}, s32[]{:T(128)}, f32[3,64]{1,0:T(4,128)S(1)}, /*index=5*/f32[64]{0:T(128)S(1)}, ...), branch_computations={%region_1.1_spmd, %region_2.7_spmd} | conditional | flops 394092832 | bytes 23842928 | solution.py:143
  66.5 5.0 %multiply_convert_fusion = (bf16[64,64,128]{2,1,0:T(8,128)(2,1)S(1)}, f32[64,64,128]{2,1,0:T(8,128)}) fusion(f32[64,128]{1,0:T(8,128)S(1)} %get-tuple-element.606, f32[64,128]{1,0:T(8,128)S(1)} %get-tuple-element.605, f32[8,128]{1,0:T(8,128)S(1)} %get-tuple-element.613, f32[8]{0:T(128)S(1)} %convert_multiply_fusion.2, f32[64,64]{1,0:T(8,128)S(1)} %copy.36), kind=kOutput, calls=%fused_computation.16 | convolution fusion | flops 54132736 | bytes 3231776 | tf_op jit(solution)/shard_map/while/body/eval_jaxpr/cond/branch_1_fun/jvp(ijm,mc->ijc)/dot_general | solution.py:51
  72.0 1.2 convolution_convert_fusion
  73.6 5.5 %fusion.25 = f32[64,64]{1,0:T(8,128)S(1)} fusion(bf16[64,64,128]{2,1,0:T(8,128)(2,1)S(1)} %bitcast.41, f32[64,64,128]{2,1,0:T(8,128)S(1)} %copy-done.8, f32[64,128]{1,0:T(8,128)S(1)} %get-tuple-element.606, f32[64,128]{1,0:T(8,128)S(1)} %get-tuple-element.605, f32[8]{0:T(128)S(1)} %convert_multiply_fusion.2, f32[64,64]{1,0:T(8,128)S(1)} %copy.36, ...), kind=kOutput, calls=%fused_computation.23 | convolution fusion | flops 56946688 | bytes 3248160 | tf_op jit(solution)/shard_map/while/body/eval_jaxpr/cond/branch_1_fun/transpose(jvp(ijm,mc->ijc))/dot_general | solution.py:51
  79.2 2.3 %fusion.11 = f32[1,4096]{1,0:T(1,128)S(1)} fusion(f32[4096,128]{1,0:T(8,128)S(1)} %fusion.66, f32[128]{0:T(128)S(1)} %get-tuple-element.615), kind=kOutput, calls=%fused_computation.13 | convolution fusion | flops 8388608 | bytes 2114048 | tf_op jit(solution)/shard_map/while/body/eval_jaxpr/cond/branch_1_fun/jvp()/dot_general | solution.py:57
  84.3 17.1 %conditional.3 = (f32[64]{0:T(128)S(1)}, f32[3,64]{1,0:T(4,128)S(1)}, f32[3,64]{1,0:T(4,128)S(1)}) conditional(s32[]{:T(128)} %convert_element_type.79, () %tuple.95, (f32[64,128]{1,0:T(8,128)S(1)}, f32[64,128]{1,0:T(8,128)S(1)}, f32[3,1536]{1,0:T(4,128)S(1)}, s32[]{:T(128)}, f32[3,64]{1,0:T(4,128)S(1)}, /*index=5*/f32[64]{0:T(128)S(1)}, ...), branch_computations={%region_1.1_spmd, %region_2.7_spmd} | conditional | flops 394092832 | bytes 23842928 | solution.py:143
  85.9 5.0 %multiply_convert_fusion = (bf16[64,64,128]{2,1,0:T(8,128)(2,1)S(1)}, f32[64,64,128]{2,1,0:T(8,128)}) fusion(f32[64,128]{1,0:T(8,128)S(1)} %get-tuple-element.606, f32[64,128]{1,0:T(8,128)S(1)} %get-tuple-element.605, f32[8,128]{1,0:T(8,128)S(1)} %get-tuple-element.613, f32[8]{0:T(128)S(1)} %convert_multiply_fusion.2, f32[64,64]{1,0:T(8,128)S(1)} %copy.36), kind=kOutput, calls=%fused_computation.16 | convolution fusion | flops 54132736 | bytes 3231776 | tf_op jit(solution)/shard_map/while/body/eval_jaxpr/cond/branch_1_fun/jvp(ijm,mc->ijc)/dot_general | solution.py:51
  91.5 1.2 convolution_convert_fusion
  93.1 5.5 %fusion.25 = f32[64,64]{1,0:T(8,128)S(1)} fusion(bf16[64,64,128]{2,1,0:T(8,128)(2,1)S(1)} %bitcast.41, f32[64,64,128]{2,1,0:T(8,128)S(1)} %copy-done.8, f32[64,128]{1,0:T(8,128)S(1)} %get-tuple-element.606, f32[64,128]{1,0:T(8,128)S(1)} %get-tuple-element.605, f32[8]{0:T(128)S(1)} %convert_multiply_fusion.2, f32[64,64]{1,0:T(8,128)S(1)} %copy.36, ...), kind=kOutput, calls=%fused_computation.23 | convolution fusion | flops 56946688 | bytes 3248160 | tf_op jit(solution)/shard_map/while/body/eval_jaxpr/cond/branch_1_fun/transpose(jvp(ijm,mc->ijc))/dot_general | solution.py:51
  98.7 2.3 %fusion.11 = f32[1,4096]{1,0:T(1,128)S(1)} fusion(f32[4096,128]{1,0:T(8,128)S(1)} %fusion.66, f32[128]{0:T(128)S(1)} %get-tuple-element.615), kind=kOutput, calls=%fused_computation.13 | convolution fusion | flops 8388608 | bytes 2114048 | tf_op jit(solution)/shard_map/while/body/eval_jaxpr/cond/branch_1_fun/jvp()/dot_general | solution.py:57
  106.4 20.3 %collective-permute-start.2 = (f32[3,512]{1,0:T(4,128)S(1)}, f32[3,512]{1,0:T(4,128)S(1)}, u32[]{:S(2)}, u32[]{:S(2)}) collective-permute-start(f32[3,512]{1,0:T(4,128)S(1)} %get-tuple-element.822), channel_id=1, source_target_pairs={{0,8},{8,16},{16,24},{24,32},{32,40},{40,48},{48,56},{56,64},{64,7... | collective-permute-start | bytes 18440 | tf_op jit(solution)/shard_map/ppermute | solution.py:26
  126.7 1.9 collective-permute-start.3
  128.7 1.3 collective-permute-done.3
  130.0 0.9 copy.45
  130.9 69.7 %reduce-scatter.4.cloned.1.call-done = f32[64,3]{1,0:T(8,128)} async-done(((f32[512,3]{1,0:T(8,128)}), f32[64,3]{1,0:T(8,128)}) %reduce-scatter.4.cloned.1.call-update) | async-done | bytes 784
  200.6 0.8 copy.46
  (110 shorter events, 12.1 us)
Async XLA Ops:
  7.2 1.6 copy-start
  7.2 193.4 %reduce-scatter.4.cloned.1.call-start = ((), (), s32[]{:S(2)}) async-start(), calls=%async_computation.1 | async-start | bytes 294912
  39.8 11.5 %collective-permute-start = (f32[132,512]{0,1:T(8,128)S(1)}, f32[132,512]{0,1:T(8,128)S(1)}, u32[]{:S(2)}, u32[]{:S(2)}) collective-permute-start(f32[132,512]{0,1:T(8,128)S(1)} %all_gather.3), channel_id=1, source_target_pairs={{0,8},{8,16},{16,24},{24,32},{32,40},{40,48},{48,56},{56,64},{64,7... | collective-permute-start | bytes 811016 | tf_op jit(solution)/shard_map/ppermute | solution.py:15
  41.7 19.9 %collective-permute-start.1 = (f32[132,512]{0,1:T(8,128)S(1)}, f32[132,512]{0,1:T(8,128)S(1)}, u32[]{:S(2)}, u32[]{:S(2)}) collective-permute-start(f32[132,512]{0,1:T(8,128)S(1)} %all_gather.3), channel_id=1, source_target_pairs={{8,0},{16,8},{24,16},{32,24},{40,32},{48,40},{56,48},{64,56},{72,6... | collective-permute-start | bytes 811016 | tf_op jit(solution)/shard_map/ppermute | solution.py:18
  61.6 1.2 copy-start.1
  61.6 1.2 copy-start.2
  61.6 1.2 copy-start.4
  61.6 1.2 copy-start.5
  61.7 1.2 copy-start.6
  61.7 1.2 copy-start.7
  72.0 1.6 copy-start.8
  91.5 1.6 copy-start.8
  106.4 95.7 %copy-start.3 = (f32[64]{0:T(128)}, f32[64]{0:T(128)S(1)}, u32[]{:S(2)}) copy-start(f32[64]{0:T(128)S(1)} %get-tuple-element.645) | copy-start | bytes 772
  106.4 22.3 %collective-permute-start.2 = (f32[3,512]{1,0:T(4,128)S(1)}, f32[3,512]{1,0:T(4,128)S(1)}, u32[]{:S(2)}, u32[]{:S(2)}) collective-permute-start(f32[3,512]{1,0:T(4,128)S(1)} %get-tuple-element.822), channel_id=1, source_target_pairs={{0,8},{8,16},{16,24},{24,32},{32,40},{40,48},{48,56},{56,64},{64,7... | collective-permute-start | bytes 18440 | tf_op jit(solution)/shard_map/ppermute | solution.py:26
  126.7 3.3 %collective-permute-start.3 = (f32[3,512]{1,0:T(4,128)S(1)}, f32[3,512]{1,0:T(4,128)S(1)}, u32[]{:S(2)}, u32[]{:S(2)}) collective-permute-start(f32[3,512]{1,0:T(4,128)S(1)} %get-tuple-element.823), channel_id=1, source_target_pairs={{0,760},{8,0},{16,8},{24,16},{32,24},{40,32},{48,40},{56,48},{64,5... | collective-permute-start | bytes 18440 | tf_op jit(solution)/shard_map/ppermute | solution.py:26
Sparse Core Ops, SparseCore 0:
  131.0 69.5 reduce-scatter.3
where the time goes:
time: 210 us; the launch traced here: 209 us
  waiting for transfers between devices  85.4 us (41%)
  matrix products  31.3 us (15%)
  blocking collectives  30 us (14%)
  starting transfers between devices  28.8 us (14%)
  between operations  14.2 us (7%)
  local copies, waits for them, and re-layouts  9.54 us (5%)
  loops' own time  7.16 us (3%)
  other arithmetic  2.47 us (1%)
    unnamed x2, waiting for transfers between devices  69.7 us
    all_gather x1, blocking collectives, per_device(): block_strip = lax.all_gather(loop_carry_state, 'grp', axis=1, tiled=True)  30 us
    ppermute x2, starting transfers between devices, from_behind(): return lax.ppermute(value, axis, pairs)  22.3 us
    dot_general x4, matrix products, pair_tile(): jnp.einsum('ijm,mc->ijc', basis, radial, precision=lax.Precision.HIGHEST)  21 us
    ppermute x1, waiting for transfers between devices, with_halo(): lax.ppermute(lax.slice_in_dim(block, 0, width, axis=dim), axis, backward)  10.2 us
    another operation x1, loops' own time, per_device(): energy, own_grad, win_grad = lax.fori_loop(0, nblk * tiles, step, start)  5.54 us
    dot_general x2, matrix products, pair_tile(): jnp.dot(mixed, readout, precision=lax.Precision.HIGHEST)  4.57 us
    ppermute x1, starting transfers between devices, with_halo(): lax.ppermute(lax.slice_in_dim(block, 0, width, axis=dim), axis, backward)  4.54 us
  transfers between devices with their start and end apart: 5, of which 4 were waited for; matrix products, arithmetic and copies ran while one was open for 0% of the time, Pallas kernels for 0%

commit v1 on v0

v1 whole, which is shorter than its diff:
```python
import functools

import jax
import jax.numpy as jnp
from jax import lax
from jax.experimental import pallas as pl
from jax.experimental.pallas import tpu as pltpu
from jax.sharding import PartitionSpec as P

BLOCK = 64
C = 128
ROWS = 72
PAIRS = BLOCK * BLOCK
CHUNK = 512
SPACING = 2.5 / 7
MESH = pl.DeviceIdType.MESH
BF16, F32 = jnp.bfloat16, jnp.float32


def parts(value, count):
    found = []
    for _ in range(count):
        part = value.astype(BF16).astype(F32)
        found.append(part)
        value = value - part
    return found


def dot(left, right):
    return jnp.dot(left, right, preferred_element_type=F32)


def centre_onehot(start, width):
    lane = lax.broadcasted_iota(jnp.int32, (BLOCK, width), 1) + start
    row = lax.broadcasted_iota(jnp.int32, (BLOCK, width), 0)
    return jnp.where((lane // BLOCK) == row, 1.0, 0.0).astype(F32)


def kernel(
    slabs,
    members,
    pos_ref,
    spc_ref,
    node_ref,
    wself_ref,
    wsend_ref,
    radial_ref,
    wmix_ref,
    readout_ref,
    scale_ref,
    nbr_ref,
    count_ref,
    energy_ref,
    force_ref,
    own,
    sib,
    far,
    cur,
    self_exp,
    pos_exp,
    scale_exp,
    rhs_tail,
    lhs_z,
    lhs_b,
    lhs_r,
    lhs_m,
    ro_exp,
    pair_acc,
    tile_acc,
    grads,
    back,
    send_sem,
    recv_sem,
    back_send_sem,
    back_recv_sem,
):
    slab, me = lax.axis_index("slab"), lax.axis_index("grp")
    core = lax.rem(slab, 2)
    sib_slab = slab + 1 - 2 * core
    far_slab = lax.rem(slab - 1 + 2 * core + slabs, slabs)
    sib_panel, far_panel = 2 - 2 * core, 2 * core

    barrier = pltpu.get_barrier_semaphore()
    for k in range(members):
        to = lax.rem(me + k, members)
        pl.semaphore_signal(barrier, inc=1, device_id=(sib_slab, to), device_id_type=MESH)
        pl.semaphore_signal(barrier, inc=1, device_id=(far_slab, to), device_id_type=MESH)
        if k:
            pl.semaphore_signal(barrier, inc=1, device_id=(slab, to), device_id_type=MESH)

    species = spc_ref[...].astype(F32).reshape(1, BLOCK)
    own[me, 0:BLOCK, :] = dot(node_ref[...], wsend_ref[...])
    pad = jnp.zeros((1, BLOCK), F32)
    place = jnp.concatenate([pos_ref[...], species, pad, pad, pad, pad], axis=0)
    own[me, BLOCK:ROWS, :] = jnp.concatenate([place, jnp.zeros_like(place)], axis=1)

    pl.semaphore_wait(barrier, 3 * members - 1)

    def send(panel, index, to_slab, to):
        pltpu.make_async_remote_copy(
            src_ref=own.at[me],
            dst_ref=panel.at[me],
            send_sem=send_sem,
            recv_sem=recv_sem.at[index],
            device_id=(to_slab, to),
            device_id_type=MESH,
        ).start()

    for k in range(members):
        send(sib, 0, sib_slab, lax.rem(me + k, members))
    for k in range(members):
        send(far, 1, far_slab, lax.rem(me + k, members))
    for k in range(1, members):
        send(own, 2, slab, lax.rem(me + k, members))

    row8 = lax.broadcasted_iota(jnp.int32, (8, BLOCK), 0)
    scale8 = jnp.zeros((8, BLOCK), F32)
    for r in range(4):
        for s in range(4):
            scale8 = jnp.where((row8 == s) & (species == float(r)), scale_ref[r, s], scale8)
    small = jnp.concatenate(parts(place, 3) + parts(scale8, 3), axis=0).astype(BF16)
    self_feat = dot(node_ref[...], wself_ref[...]) * 0.5
    self_t = jnp.concatenate(parts(self_feat, 2), axis=0).T.astype(BF16)

    def expand(step, carry):
        lanes = pl.ds(pl.multiple_of(step * CHUNK, CHUNK), CHUNK)
        hot = centre_onehot(step * CHUNK, CHUNK)
        spread = dot(small, hot.astype(BF16))
        pos_exp[:, lanes] = spread[0:8] + spread[8:16] + spread[16:24]
        scale_exp[:, lanes] = spread[24:32] + spread[32:40] + spread[40:48]
        self_exp[:, lanes] = dot(self_t, jnp.concatenate([hot, hot], axis=0).astype(BF16))
        return carry

    lax.fori_loop(0, PAIRS // CHUNK, expand, 0)

    atom = lax.broadcasted_iota(jnp.int32, (BLOCK, CHUNK), 0)
    lane = lax.broadcasted_iota(jnp.int32, (BLOCK, CHUNK), 1)
    hot_j = jnp.where(lax.rem(lane, BLOCK) == atom, 1.0, 0.0).astype(F32)
    rhs_tail[...] = jnp.concatenate([hot_j, hot_j], axis=0).astype(BF16)

    radial_hi, radial_lo = parts(radial_ref[...], 2)
    lhs_r[...] = (jnp.concatenate([radial_hi, radial_lo], axis=0) * 0.25).astype(BF16)
    lhs_m[...] = (wmix_ref[...].astype(F32).T * 0.5).astype(BF16)
    ones = jnp.ones((16, C), F32)
    lhs_b[...] = jnp.concatenate(
        [
            jnp.concatenate([jnp.zeros((C, C), F32), ones], axis=0),
            jnp.concatenate([wmix_ref[...].astype(F32), jnp.zeros((16, C), F32)], axis=0),
        ],
        axis=1,
    ).astype(BF16)
    readout = readout_ref[...].reshape(1, C)
    ro_exp[...] = jnp.broadcast_to(readout, (C, C)).T
    pair_acc[...] = jnp.zeros_like(pair_acc)
    grads[...] = jnp.zeros_like(grads)

    center = lax.broadcasted_iota(jnp.int32, (8, CHUNK), 0).astype(F32) * SPACING
    row = lax.broadcasted_iota(jnp.int32, (8, CHUNK), 0)
    pair = lax.broadcasted_iota(jnp.int32, (8, CHUNK), 1)

    def tile(turn, carry):
        slot = jnp.where(turn == 0, 1 - core, jnp.where(turn == 1, core, turn))
        other = nbr_ref[0, slot]
        panel, member = other // members, lax.rem(other, members)

        @pl.when(turn == 0)
        def _():
            pltpu.make_async_copy(sib, sib, recv_sem.at[0]).wait()
            cur[...] = sib[member]

        @pl.when(turn == 1)
        def _():
            pltpu.make_async_copy(far, far, recv_sem.at[1]).wait()
            cur[...] = far[member]

        @pl.when(turn == 2)
        def _():
            some = own.at[pl.ds(0, members - 1)]
            pltpu.make_async_copy(some, some, recv_sem.at[2]).wait()

        @pl.when(turn >= 2)
        def _():
            cur[...] = jnp.where(
                panel == sib_panel,
                sib[member],
                jnp.where(panel == far_panel, far[member], own[member]),
            )

        live = jnp.where(slot < count_ref[0], 1.0, 0.0)
        same = (panel == 1) & (member == me)
        place_j = cur[BLOCK:ROWS, 0:BLOCK]
        place_j = jnp.concatenate([place_j] * (CHUNK // BLOCK), axis=1)
        kind_j = jnp.broadcast_to(place_j[3:4], (8, CHUNK))
        kind_hot = jnp.where(kind_j == row.astype(F32), 1.0, 0.0)
        send_hi, send_lo = parts(cur[0:BLOCK, :] * 0.5, 2)
        half_hi, half_lo = parts(radial_ref[...] * 0.5, 2)
        lhs_z[...] = jnp.concatenate(
            [half_hi, half_lo, half_hi, jnp.zeros((8, C), F32), send_hi, send_lo], axis=0
        ).T.astype(BF16)
        tile_acc[...] = jnp.zeros_like(tile_acc)

        def step(index, carry):
            start = pl.multiple_of(index * CHUNK, CHUNK)
            lanes = pl.ds(start, CHUNK)
            diff = jnp.where(row < 3, place_j - pos_exp[:, lanes], 0.0)
            dist_sq = jnp.sum(diff * diff, axis=0, keepdims=True)
            scale = jnp.sum(scale_exp[:, lanes] * kind_hot, axis=0, keepdims=True)
            scaled = dist_sq * scale
            centre = (pair + start) // BLOCK
            keep = jnp.where(same & (centre == lax.rem(pair, BLOCK)), 0.0, live)[0:1]
            reach = jnp.maximum(1.0 - scaled / 2.5, 0.0)
            cut = reach * reach
            offset = (scaled - center) / SPACING
            basis = jnp.exp(-(offset * offset))
            slope = basis * offset * (-2.0 / SPACING)
            basis_hi, basis_lo = parts(basis, 2)
            head = jnp.concatenate(
                [basis_hi, basis_hi, basis_lo, jnp.zeros((8, CHUNK), F32)], axis=0
            ).astype(BF16)
            rhs = jnp.concatenate([head, rhs_tail[...]], axis=0)
            half = dot(lhs_z[...], rhs) + self_exp[:, lanes]
            t = jnp.tanh(half)
            p = 1.0 + t
            hidden = half * p
            slope_1 = p * (1.0 + half * (1.0 - t))
            half = dot(lhs_m[...], hidden.astype(BF16))
            t = jnp.tanh(half)
            p = (1.0 + t) * jnp.concatenate([ro_exp[...]] * (CHUNK // C), axis=1)
            mixed = half * p
            slope_2 = p * (1.0 + half * (1.0 - t))
            out = dot(lhs_b[...], jnp.concatenate([mixed, slope_2], axis=0).astype(BF16))
            d_latent = out[0:C] * slope_1
            d_basis = dot(lhs_r[...], d_latent.astype(BF16))
            d_basis = d_basis[0:8] + d_basis[8:16]
            energy = out[C : C + 1]
            d_scaled = cut * jnp.sum(d_basis * slope, axis=0, keepdims=True)
            d_scaled = d_scaled - (2.0 / 2.5) * reach * energy
            force = (2.0 * keep * scale * d_scaled) * diff
            found = jnp.where(row == 3, keep * cut * energy, force)
            pair_acc[:, lanes] += found
            total = found[:, 0:C]
            for k in range(1, CHUNK // C):
                total = total + found[:, k * C : (k + 1) * C]
            tile_acc[...] += total
            return carry

        lax.fori_loop(0, PAIRS // CHUNK, step, 0)
        grad = tile_acc[:, 0:BLOCK] + tile_acc[:, BLOCK:C]
        grad = jnp.concatenate([grad, jnp.zeros_like(grad)], axis=1)
        group = jnp.where(panel == sib_panel, 0, jnp.where(panel == far_panel, 1, 2))
        which = group * members + member
        for k in range(3 * members):
            grads[k] += jnp.where(which == k, grad, 0.0)
        return carry

    lax.fori_loop(0, 4, tile, 0)

    def give(index, to_slab, to):
        pltpu.make_async_remote_copy(
            src_ref=grads.at[index * members + to],
            dst_ref=back.at[index * members + me],
            send_sem=back_send_sem,
            recv_sem=back_recv_sem,
            device_id=(to_slab, to),
            device_id_type=MESH,
        ).start()

    for k in range(members):
        give(1, far_slab, lax.rem(me + k, members))
    for k in range(1, members):
        give(2, slab, lax.rem(me + k, members))
    for k in range(members):
        give(0, sib_slab, lax.rem(me + k, members))
    back[2 * members + me] = grads[2 * members + me]

    def gather(index, total):
        lanes = pl.ds(pl.multiple_of(index * CHUNK, CHUNK), CHUNK)
        split = jnp.concatenate(parts(pair_acc[:, lanes], 3), axis=0).astype(BF16)
        hot = centre_onehot(index * CHUNK, CHUNK).astype(BF16)
        found = lax.dot_general(
            split, hot, (((1,), (1,)), ((), ())), preferred_element_type=F32
        )
        return total + (found[0:8] + found[8:16] + found[16:24])

    centre_sum = lax.fori_loop(0, PAIRS // CHUNK, gather, jnp.zeros((8, BLOCK), F32))
    energy_ref[...] = centre_sum[3:4].reshape(BLOCK)

    some = back.at[pl.ds(0, 3 * members - 1)]
    pltpu.make_async_copy(some, some, back_recv_sem).wait()
    total = back[0]
    for k in range(1, 3 * members):
        total = total + back[k]
    force_ref[...] = centre_sum[0:3] - total[0:3, 0:BLOCK]

    for panel in (sib, far, own.at[pl.ds(0, members - 1)]):
        pltpu.make_async_copy(panel, panel, send_sem).wait()
    pltpu.make_async_copy(some, some, back_send_sem).wait()


def solution(mesh):
    slabs, members = mesh.shape["slab"], mesh.shape["grp"]
    vmem = pl.BlockSpec(memory_space=pltpu.VMEM)
    smem = pl.BlockSpec(memory_space=pltpu.SMEM)
    panel = pltpu.VMEM((members, ROWS, C), F32)
    call = pl.pallas_call(
        functools.partial(kernel, slabs, members),
        out_shape=(
            jax.ShapeDtypeStruct((BLOCK,), F32),
            jax.ShapeDtypeStruct((3, BLOCK), F32),
        ),
        in_specs=[vmem] * 8 + [smem] * 3,
        out_specs=(vmem, vmem),
        scratch_shapes=[
            panel,
            panel,
            panel,
            pltpu.VMEM((ROWS, C), F32),
            pltpu.VMEM((C, PAIRS), F32),
            pltpu.VMEM((8, PAIRS), F32),
            pltpu.VMEM((8, PAIRS), F32),
            pltpu.VMEM((2 * BLOCK, CHUNK), BF16),
            pltpu.VMEM((C, 160), BF16),
            pltpu.VMEM((C + 16, 2 * C), BF16),
            pltpu.VMEM((16, C), BF16),
            pltpu.VMEM((C, C), BF16),
            pltpu.VMEM((C, C), F32),
            pltpu.VMEM((8, PAIRS), F32),
            pltpu.VMEM((8, C), F32),
            pltpu.VMEM((3 * members, 8, C), F32),
            pltpu.VMEM((3 * members, 8, C), F32),
            pltpu.SemaphoreType.DMA,
            pltpu.SemaphoreType.DMA((3,)),
            pltpu.SemaphoreType.DMA,
            pltpu.SemaphoreType.DMA,
        ],
        compiler_params=pltpu.CompilerParams(
            collective_id=0, has_side_effects=True, vmem_limit_bytes=48 * 2**20
        ),
    )
    return jax.shard_map(
        call,
        mesh=mesh,
        in_specs=(
            P(None, ("slab", "grp")),
            P(("slab", "grp")),
            P(("slab", "grp"), None),
            P(),
            P(),
            P(),
            P(),
            P(),
            P(),
            P(("slab", "grp"), None),
            P(("slab", "grp")),
        ),
        out_specs=(P(("slab", "grp")), P(None, ("slab", "grp"))),
        check_vma=False,
    )
```

time: 210 us -> 68.7 us (0.33)
  the two profiles are of different devices: /device:TPU:16 before, /device:TPU:8 now
where the time goes in v1:
time: 68.7 us; the launch traced here: 68.2 us
  Pallas kernels  60.7 us (88%)
  local copies, waits for them, and re-layouts  6.13 us (9%)
  between operations  1.37 us (2%)
    pallas_call x1, Pallas kernels  60.7 us
    unnamed x22, local copies, waits for them, and re-layouts  6.13 us

profile of v1, /device:TPU:8, one launch (start us, length us, event | category | flops | bytes accessed | tf_op | source)
XLA Modules:
  0.0 68.2 jit_solution(5675745614601205369)
XLA Ops:
  0.6 0.0 copy-start.9
  0.6 0.0 copy-start.8
  0.7 0.0 copy-start.7
  1.3 0.0 copy-done.9
  1.3 0.0 copy-done.8
  1.4 0.0 copy-done.7
  1.4 0.0 copy-start
  1.4 0.7 %copy-done = bf16[128,128]{1,0:T(8,128)(2,1)S(1)} copy-done((bf16[128,128]{1,0:T(8,128)(2,1)S(1)}, bf16[128,128]{1,0:T(8,128)(2,1)}, u32[]{:S(2)}) %copy-start) | copy-done | bytes 32792
  2.1 0.0 copy-start.1
  2.1 0.8 %copy-done.1 = bf16[128,128]{1,0:T(8,128)(2,1)S(1)} copy-done((bf16[128,128]{1,0:T(8,128)(2,1)S(1)}, bf16[128,128]{1,0:T(8,128)(2,1)}, u32[]{:S(2)}) %copy-start.1) | copy-done | bytes 32792
  2.9 0.0 copy-start.2
  2.9 0.8 %copy-done.2 = bf16[128,128]{1,0:T(8,128)(2,1)S(1)} copy-done((bf16[128,128]{1,0:T(8,128)(2,1)S(1)}, bf16[128,128]{1,0:T(8,128)(2,1)}, u32[]{:S(2)}) %copy-start.2) | copy-done | bytes 32792
  3.6 0.0 copy-start.3
  3.6 0.7 %copy-done.3 = bf16[64,128]{1,0:T(8,128)(2,1)S(1)} copy-done((bf16[64,128]{1,0:T(8,128)(2,1)S(1)}, bf16[64,128]{1,0:T(8,128)(2,1)}, u32[]{:S(2)}) %copy-start.3) | copy-done | bytes 16408
  4.4 0.0 copy-start.4
  4.4 0.7 %copy-done.4 = f32[8,128]{1,0:T(8,128)S(1)} copy-done((f32[8,128]{1,0:T(8,128)S(1)}, f32[8,128]{1,0:T(8,128)}, u32[]{:S(2)}) %copy-start.4) | copy-done | bytes 4120
  5.0 0.0 copy-start.5
  5.0 0.7 copy-done.5
  5.7 0.0 copy-start.6
  5.7 0.7 copy-done.6
  6.4 60.7 %shard_map.122 = (f32[64]{0:T(128)S(1)}, f32[3,64]{1,0:T(4,128)S(1)}) custom-call(f32[3,64]{1,0:T(4,128)S(1)} %copy-done.5, s32[64]{0:T(128)S(1)} %copy-done.7, bf16[64,128]{1,0:T(8,128)(2,1)S(1)} %copy-done.3, bf16[128,128]{1,0:T(8,128)(2,1)S(1)} %copy-done, bf16[128,128]{1,0:T(8,128)(2,1)S(1)} %copy-done.1, f32[8,128]{1,0:T(8,128)S(1)} %copy-done.4, ...), custom_call_target="tpu_custom_call" | custom-call | tf_op jit(solution)/shard_map/pallas_call
  67.1 0.5 copy.16
  67.6 0.6 copy.17
Async XLA Ops:
  0.6 0.7 %copy-start.9 = (s32[1,4]{1,0:T(1,128)S(1)}, s32[1,4]{1,0:T(1,128)}, u32[]{:S(2)}) copy-start(s32[1,4]{1,0:T(1,128)} %nbr_ref.1) | copy-start | bytes 52
  0.6 0.7 %copy-start.8 = (f32[128]{0:T(128)S(1)}, f32[128]{0:T(128)}, u32[]{:S(2)}) copy-start(f32[128]{0:T(128)} %readout_ref.1) | copy-start | bytes 1540
  0.7 0.7 %copy-start.7 = (s32[64]{0:T(128)S(1)}, s32[64]{0:T(128)}, u32[]{:S(2)}) copy-start(s32[64]{0:T(128)} %spc_ref.1) | copy-start | bytes 772
  1.4 0.8 %copy-start = (bf16[128,128]{1,0:T(8,128)(2,1)S(1)}, bf16[128,128]{1,0:T(8,128)(2,1)}, u32[]{:S(2)}) copy-start(bf16[128,128]{1,0:T(8,128)(2,1)} %wself_ref.1) | copy-start | bytes 98308
  2.1 0.8 %copy-start.1 = (bf16[128,128]{1,0:T(8,128)(2,1)S(1)}, bf16[128,128]{1,0:T(8,128)(2,1)}, u32[]{:S(2)}) copy-start(bf16[128,128]{1,0:T(8,128)(2,1)} %wsend_ref.1) | copy-start | bytes 98308
  2.9 0.8 %copy-start.2 = (bf16[128,128]{1,0:T(8,128)(2,1)S(1)}, bf16[128,128]{1,0:T(8,128)(2,1)}, u32[]{:S(2)}) copy-start(bf16[128,128]{1,0:T(8,128)(2,1)} %wmix_ref.1) | copy-start | bytes 98308
  3.6 0.7 %copy-start.3 = (bf16[64,128]{1,0:T(8,128)(2,1)S(1)}, bf16[64,128]{1,0:T(8,128)(2,1)}, u32[]{:S(2)}) copy-start(bf16[64,128]{1,0:T(8,128)(2,1)} %node_ref.1) | copy-start | bytes 49156
  4.4 0.7 %copy-start.4 = (f32[8,128]{1,0:T(8,128)S(1)}, f32[8,128]{1,0:T(8,128)}, u32[]{:S(2)}) copy-start(f32[8,128]{1,0:T(8,128)} %radial_ref.1) | copy-start | bytes 12292
  5.0 0.7 copy-start.5
  5.7 0.7 copy-start.6

commit v2 on v1

--- a/solution.py
+++ b/solution.py
@@ -11,7 +11,9 @@
 C = 128
 ROWS = 72
 PAIRS = BLOCK * BLOCK
-CHUNK = 512
+CHUNK = 1024
+CENTRES = CHUNK // BLOCK
+UNROLL = 4
 SPACING = 2.5 / 7
 MESH = pl.DeviceIdType.MESH
 BF16, F32 = jnp.bfloat16, jnp.float32
@@ -39,6 +41,19 @@
 def kernel(
     slabs,
     members,
+    pos_hbm,
+    spc_hbm,
+    node_hbm,
+    wself_hbm,
+    wsend_hbm,
+    radial_hbm,
+    wmix_hbm,
+    readout_hbm,
+    scale_hbm,
+    nbr_hbm,
+    count_hbm,
+    energy_ref,
+    force_ref,
     pos_ref,
     spc_ref,
     node_ref,
@@ -50,25 +65,24 @@
     scale_ref,
     nbr_ref,
     count_ref,
-    energy_ref,
-    force_ref,
     own,
     sib,
     far,
     cur,
-    self_exp,
     pos_exp,
     scale_exp,
-    rhs_tail,
-    lhs_z,
+    rhs_pair,
+    rhs_centre,
+    lhs_send,
+    lhs_rest,
     lhs_b,
     lhs_r,
     lhs_m,
     ro_exp,
     pair_acc,
-    tile_acc,
     grads,
     back,
+    load_sem,
     send_sem,
     recv_sem,
     back_send_sem,
@@ -83,10 +97,35 @@
     barrier = pltpu.get_barrier_semaphore()
     for k in range(members):
         to = lax.rem(me + k, members)
+        pl.semaphore_signal(barrier, inc=1, device_id=(far_slab, to), device_id_type=MESH)
+    for k in range(members):
+        to = lax.rem(me + k, members)
         pl.semaphore_signal(barrier, inc=1, device_id=(sib_slab, to), device_id_type=MESH)
-        pl.semaphore_signal(barrier, inc=1, device_id=(far_slab, to), device_id_type=MESH)
         if k:
             pl.semaphore_signal(barrier, inc=1, device_id=(slab, to), device_id_type=MESH)
+
+    loads = [
+        pltpu.make_async_copy(source, target, load_sem.at[k])
+        for k, (source, target) in enumerate(
+            [
+                (node_hbm, node_ref),
+                (wsend_hbm, wsend_ref),
+                (pos_hbm, pos_ref),
+                (spc_hbm, spc_ref),
+                (wself_hbm, wself_ref),
+                (radial_hbm, radial_ref),
+                (wmix_hbm, wmix_ref),
+                (readout_hbm, readout_ref),
+                (scale_hbm, scale_ref),
+                (nbr_hbm, nbr_ref),
+                (count_hbm, count_ref),
+            ]
+        )
+    ]
+    for load in loads:
+        load.start()
+    for load in loads[:4]:
+        load.wait()
 
     species = spc_ref[...].astype(F32).reshape(1, BLOCK)
     own[me, 0:BLOCK, :] = dot(node_ref[...], wsend_ref[...])
@@ -107,28 +146,32 @@
         ).start()
 
     for k in range(members):
+        send(far, 1, far_slab, lax.rem(me + k, members))
+    for k in range(members):
         send(sib, 0, sib_slab, lax.rem(me + k, members))
-    for k in range(members):
-        send(far, 1, far_slab, lax.rem(me + k, members))
     for k in range(1, members):
         send(own, 2, slab, lax.rem(me + k, members))
 
+    for load in loads[4:]:
+        load.wait()
     row8 = lax.broadcasted_iota(jnp.int32, (8, BLOCK), 0)
     scale8 = jnp.zeros((8, BLOCK), F32)
     for r in range(4):
         for s in range(4):
             scale8 = jnp.where((row8 == s) & (species == float(r)), scale_ref[r, s], scale8)
     small = jnp.concatenate(parts(place, 3) + parts(scale8, 3), axis=0).astype(BF16)
-    self_feat = dot(node_ref[...], wself_ref[...]) * 0.5
-    self_t = jnp.concatenate(parts(self_feat, 2), axis=0).T.astype(BF16)
+    half_hi, half_lo = parts(radial_ref[...] * 0.5, 2)
+    self_hi, self_lo = parts(dot(node_ref[...], wself_ref[...]) * 0.5, 2)
+    for k in range(PAIRS // CHUNK):
+        mine = slice(k * CENTRES, (k + 1) * CENTRES)
+        rest = [half_hi, half_lo, half_hi, jnp.zeros((8, C), F32), self_hi[mine], self_lo[mine]]
+        lhs_rest[k] = jnp.concatenate(rest, axis=0).T.astype(BF16)
 
     def expand(step, carry):
         lanes = pl.ds(pl.multiple_of(step * CHUNK, CHUNK), CHUNK)
-        hot = centre_onehot(step * CHUNK, CHUNK)
-        spread = dot(small, hot.astype(BF16))
+        spread = dot(small, centre_onehot(step * CHUNK, CHUNK).astype(BF16))
         pos_exp[:, lanes] = spread[0:8] + spread[8:16] + spread[16:24]
         scale_exp[:, lanes] = spread[24:32] + spread[32:40] + spread[40:48]
-        self_exp[:, lanes] = dot(self_t, jnp.concatenate([hot, hot], axis=0).astype(BF16))
         return carry
 
     lax.fori_loop(0, PAIRS // CHUNK, expand, 0)
@@ -136,7 +179,9 @@
     atom = lax.broadcasted_iota(jnp.int32, (BLOCK, CHUNK), 0)
     lane = lax.broadcasted_iota(jnp.int32, (BLOCK, CHUNK), 1)
     hot_j = jnp.where(lax.rem(lane, BLOCK) == atom, 1.0, 0.0).astype(F32)
-    rhs_tail[...] = jnp.concatenate([hot_j, hot_j], axis=0).astype(BF16)
+    rhs_pair[...] = jnp.concatenate([hot_j, hot_j], axis=0).astype(BF16)
+    hot_i = centre_onehot(0, CHUNK)[0:CENTRES]
+    rhs_centre[...] = jnp.concatenate([hot_i, hot_i], axis=0).astype(BF16)
 
     radial_hi, radial_lo = parts(radial_ref[...], 2)
     lhs_r[...] = (jnp.concatenate([radial_hi, radial_lo], axis=0) * 0.25).astype(BF16)
@@ -154,9 +199,10 @@
     pair_acc[...] = jnp.zeros_like(pair_acc)
     grads[...] = jnp.zeros_like(grads)
 
-    center = lax.broadcasted_iota(jnp.int32, (8, CHUNK), 0).astype(F32) * SPACING
     row = lax.broadcasted_iota(jnp.int32, (8, CHUNK), 0)
-    pair = lax.broadcasted_iota(jnp.int32, (8, CHUNK), 1)
+    pair = lax.broadcasted_iota(jnp.int32, (1, CHUNK), 1)
+    center = row.astype(F32) * SPACING
+    gap = lax.rem(pair, BLOCK) - pair // BLOCK
 
     def tile(turn, carry):
         slot = jnp.where(turn == 0, 1 - core, jnp.where(turn == 1, core, turn))
@@ -190,62 +236,78 @@
         same = (panel == 1) & (member == me)
         place_j = cur[BLOCK:ROWS, 0:BLOCK]
         place_j = jnp.concatenate([place_j] * (CHUNK // BLOCK), axis=1)
-        kind_j = jnp.broadcast_to(place_j[3:4], (8, CHUNK))
-        kind_hot = jnp.where(kind_j == row.astype(F32), 1.0, 0.0)
-        send_hi, send_lo = parts(cur[0:BLOCK, :] * 0.5, 2)
-        half_hi, half_lo = parts(radial_ref[...] * 0.5, 2)
-        lhs_z[...] = jnp.concatenate(
-            [half_hi, half_lo, half_hi, jnp.zeros((8, C), F32), send_hi, send_lo], axis=0
-        ).T.astype(BF16)
-        tile_acc[...] = jnp.zeros_like(tile_acc)
+        kind_hot = jnp.where(place_j[3:4] == row.astype(F32), 1.0, 0.0)
+        lhs_send[...] = jnp.concatenate(parts(cur[0:BLOCK, :] * 0.5, 2), axis=0).T.astype(BF16)
 
         def step(index, carry):
-            start = pl.multiple_of(index * CHUNK, CHUNK)
-            lanes = pl.ds(start, CHUNK)
-            diff = jnp.where(row < 3, place_j - pos_exp[:, lanes], 0.0)
-            dist_sq = jnp.sum(diff * diff, axis=0, keepdims=True)
-            scale = jnp.sum(scale_exp[:, lanes] * kind_hot, axis=0, keepdims=True)
-            scaled = dist_sq * scale
-            centre = (pair + start) // BLOCK
-            keep = jnp.where(same & (centre == lax.rem(pair, BLOCK)), 0.0, live)[0:1]
-            reach = jnp.maximum(1.0 - scaled / 2.5, 0.0)
-            cut = reach * reach
-            offset = (scaled - center) / SPACING
-            basis = jnp.exp(-(offset * offset))
-            slope = basis * offset * (-2.0 / SPACING)
-            basis_hi, basis_lo = parts(basis, 2)
-            head = jnp.concatenate(
-                [basis_hi, basis_hi, basis_lo, jnp.zeros((8, CHUNK), F32)], axis=0
-            ).astype(BF16)
-            rhs = jnp.concatenate([head, rhs_tail[...]], axis=0)
-            half = dot(lhs_z[...], rhs) + self_exp[:, lanes]
-            t = jnp.tanh(half)
-            p = 1.0 + t
-            hidden = half * p
-            slope_1 = p * (1.0 + half * (1.0 - t))
-            half = dot(lhs_m[...], hidden.astype(BF16))
-            t = jnp.tanh(half)
-            p = (1.0 + t) * jnp.concatenate([ro_exp[...]] * (CHUNK // C), axis=1)
-            mixed = half * p
-            slope_2 = p * (1.0 + half * (1.0 - t))
-            out = dot(lhs_b[...], jnp.concatenate([mixed, slope_2], axis=0).astype(BF16))
-            d_latent = out[0:C] * slope_1
-            d_basis = dot(lhs_r[...], d_latent.astype(BF16))
-            d_basis = d_basis[0:8] + d_basis[8:16]
-            energy = out[C : C + 1]
-            d_scaled = cut * jnp.sum(d_basis * slope, axis=0, keepdims=True)
-            d_scaled = d_scaled - (2.0 / 2.5) * reach * energy
-            force = (2.0 * keep * scale * d_scaled) * diff
-            found = jnp.where(row == 3, keep * cut * energy, force)
-            pair_acc[:, lanes] += found
-            total = found[:, 0:C]
-            for k in range(1, CHUNK // C):
-                total = total + found[:, k * C : (k + 1) * C]
-            tile_acc[...] += total
-            return carry
-
-        lax.fori_loop(0, PAIRS // CHUNK, step, 0)
-        grad = tile_acc[:, 0:BLOCK] + tile_acc[:, BLOCK:C]
+            def first(sub):
+                turn = index * UNROLL + sub
+                lanes = pl.ds(pl.multiple_of(turn * CHUNK, CHUNK), CHUNK)
+                diff = jnp.where(row < 3, place_j - pos_exp[:, lanes], 0.0)
+                dist_sq = jnp.sum(diff * diff, axis=0, keepdims=True)
+                scale = jnp.sum(scale_exp[:, lanes] * kind_hot, axis=0, keepdims=True)
+                scaled = dist_sq * scale
+                keep = jnp.where(same & (gap == turn * CENTRES), 0.0, live)
+                reach = jnp.maximum(1.0 - scaled * (1.0 / 2.5), 0.0)
+                offset = (scaled - center) * (1.0 / SPACING)
+                basis = jnp.exp(-(offset * offset))
+                slope = basis * offset * (-2.0 / SPACING)
+                basis_hi, basis_lo = parts(basis, 2)
+                head = jnp.concatenate(
+                    [basis_hi, basis_hi, basis_lo, jnp.zeros((8, CHUNK), F32)], axis=0
+                ).astype(BF16)
+                rhs = jnp.concatenate([rhs_pair[...], head, rhs_centre[...]], axis=0)
+                lhs = jnp.concatenate([lhs_send[...], lhs_rest[turn]], axis=1)
+                return lanes, diff, scale, keep, reach, slope, dot(lhs, rhs)
+
+            def second(state):
+                half = state[-1]
+                t = jnp.tanh(half)
+                p = 1.0 + t
+                hidden = half * p
+                slope_1 = p + hidden * (1.0 - t)
+                half = dot(lhs_m[...], hidden.astype(BF16))
+                return state[:-1] + (slope_1, half)
+
+            def third(state):
+                half = state[-1]
+                t = jnp.tanh(half)
+                p = (1.0 + t) * jnp.concatenate([ro_exp[...]] * (CHUNK // C), axis=1)
+                mixed = half * p
+                slope_2 = p + mixed * (1.0 - t)
+                out = dot(lhs_b[...], jnp.concatenate([mixed, slope_2], axis=0).astype(BF16))
+                return state[:-1] + (out,)
+
+            def fourth(state):
+                lanes, diff, scale, keep, reach, slope, slope_1, out = state
+                d_basis = dot(lhs_r[...], (out[0:C] * slope_1).astype(BF16))
+                d_basis = d_basis[0:8] + d_basis[8:16]
+                energy = out[C : C + 1]
+                cut = reach * reach
+                d_scaled = cut * jnp.sum(d_basis * slope, axis=0, keepdims=True)
+                d_scaled = d_scaled - (2.0 / 2.5) * reach * energy
+                force = (2.0 * keep * scale * d_scaled) * diff
+                found = jnp.where(row == 3, keep * cut * energy, force)
+                pair_acc[:, lanes] += found
+                total = found[:, 0:C]
+                for k in range(1, CHUNK // C):
+                    total = total + found[:, k * C : (k + 1) * C]
+                return total
+
+            stages = [first, second, third, fourth]
+            states = {}
+            total = carry
+            for turn in range(UNROLL + 3):
+                for depth in range(4):
+                    sub = turn - depth
+                    if 0 <= sub < UNROLL:
+                        states[sub] = stages[depth](states.get(sub, sub))
+                        if depth == 3:
+                            total = total + states.pop(sub)
+            return total
+
+        grad = lax.fori_loop(0, PAIRS // CHUNK // UNROLL, step, jnp.zeros((8, C), F32))
+        grad = grad[:, 0:BLOCK] + grad[:, BLOCK:C]
         grad = jnp.concatenate([grad, jnp.zeros_like(grad)], axis=1)
         group = jnp.where(panel == sib_panel, 0, jnp.where(panel == far_panel, 1, 2))
         which = group * members + member
@@ -300,7 +362,6 @@
 def solution(mesh):
     slabs, members = mesh.shape["slab"], mesh.shape["grp"]
     vmem = pl.BlockSpec(memory_space=pltpu.VMEM)
-    smem = pl.BlockSpec(memory_space=pltpu.SMEM)
     panel = pltpu.VMEM((members, ROWS, C), F32)
     call = pl.pallas_call(
         functools.partial(kernel, slabs, members),
@@ -308,26 +369,38 @@
             jax.ShapeDtypeStruct((BLOCK,), F32),
             jax.ShapeDtypeStruct((3, BLOCK), F32),
         ),
-        in_specs=[vmem] * 8 + [smem] * 3,
+        in_specs=[pl.BlockSpec(memory_space=pltpu.HBM)] * 11,
         out_specs=(vmem, vmem),
         scratch_shapes=[
+            pltpu.VMEM((3, BLOCK), F32),
+            pltpu.VMEM((BLOCK,), jnp.int32),
+            pltpu.VMEM((BLOCK, C), BF16),
+            pltpu.VMEM((C, C), BF16),
+            pltpu.VMEM((C, C), BF16),
+            pltpu.VMEM((8, C), F32),
+            pltpu.VMEM((C, C), BF16),
+            pltpu.VMEM((C,), F32),
+            pltpu.SMEM((4, 4), F32),
+            pltpu.SMEM((1, 4), jnp.int32),
+            pltpu.SMEM((1,), jnp.int32),
             panel,
             panel,
             panel,
             pltpu.VMEM((ROWS, C), F32),
-            pltpu.VMEM((C, PAIRS), F32),
             pltpu.VMEM((8, PAIRS), F32),
             pltpu.VMEM((8, PAIRS), F32),
             pltpu.VMEM((2 * BLOCK, CHUNK), BF16),
-            pltpu.VMEM((C, 160), BF16),
+            pltpu.VMEM((2 * CENTRES, CHUNK), BF16),
+            pltpu.VMEM((C, 2 * BLOCK), BF16),
+            pltpu.VMEM((PAIRS // CHUNK, C, 32 + 2 * CENTRES), BF16),
             pltpu.VMEM((C + 16, 2 * C), BF16),
             pltpu.VMEM((16, C), BF16),
             pltpu.VMEM((C, C), BF16),
             pltpu.VMEM((C, C), F32),
             pltpu.VMEM((8, PAIRS), F32),
-            pltpu.VMEM((8, C), F32),
             pltpu.VMEM((3 * members, 8, C), F32),
             pltpu.VMEM((3 * members, 8, C), F32),
+            pltpu.SemaphoreType.DMA((11,)),
             pltpu.SemaphoreType.DMA,
             pltpu.SemaphoreType.DMA((3,)),
             pltpu.SemaphoreType.DMA,

time: 68.7 us -> 53.3 us (0.78)
  Pallas kernels: 60.7 us -> 45.3 us
    pallas_call x1, Pallas kernels: 60.7 us -> 45.3 us
where the time goes in v2:
time: 53.3 us; the launch traced here: 52.8 us
  Pallas kernels  45.3 us (85%)
  local copies, waits for them, and re-layouts  6.13 us (12%)
  between operations  1.37 us (3%)
    pallas_call x1, Pallas kernels  45.3 us
    unnamed x22, local copies, waits for them, and re-layouts  6.13 us

profile of v2, /device:TPU:8, one launch (start us, length us, event | category | flops | bytes accessed | tf_op | source)
XLA Modules:
  0.0 52.8 jit_solution(13407338792769368611)
XLA Ops:
  0.6 0.0 copy-start.9
  0.6 0.0 copy-start.8
  0.7 0.0 copy-start.7
  1.3 0.0 copy-done.9
  1.3 0.0 copy-done.8
  1.4 0.0 copy-done.7
  1.4 0.0 copy-start
  1.4 0.7 %copy-done = bf16[128,128]{1,0:T(8,128)(2,1)S(1)} copy-done((bf16[128,128]{1,0:T(8,128)(2,1)S(1)}, bf16[128,128]{1,0:T(8,128)(2,1)}, u32[]{:S(2)}) %copy-start) | copy-done | bytes 32792
  2.1 0.0 copy-start.1
  2.1 0.8 %copy-done.1 = bf16[128,128]{1,0:T(8,128)(2,1)S(1)} copy-done((bf16[128,128]{1,0:T(8,128)(2,1)S(1)}, bf16[128,128]{1,0:T(8,128)(2,1)}, u32[]{:S(2)}) %copy-start.1) | copy-done | bytes 32792
  2.9 0.0 copy-start.2
  2.9 0.8 %copy-done.2 = bf16[128,128]{1,0:T(8,128)(2,1)S(1)} copy-done((bf16[128,128]{1,0:T(8,128)(2,1)S(1)}, bf16[128,128]{1,0:T(8,128)(2,1)}, u32[]{:S(2)}) %copy-start.2) | copy-done | bytes 32792
  3.6 0.0 copy-start.3
  3.6 0.7 %copy-done.3 = bf16[64,128]{1,0:T(8,128)(2,1)S(1)} copy-done((bf16[64,128]{1,0:T(8,128)(2,1)S(1)}, bf16[64,128]{1,0:T(8,128)(2,1)}, u32[]{:S(2)}) %copy-start.3) | copy-done | bytes 16408
  4.4 0.0 copy-start.4
  4.4 0.7 %copy-done.4 = f32[8,128]{1,0:T(8,128)S(1)} copy-done((f32[8,128]{1,0:T(8,128)S(1)}, f32[8,128]{1,0:T(8,128)}, u32[]{:S(2)}) %copy-start.4) | copy-done | bytes 4120
  5.0 0.0 copy-start.5
  5.0 0.7 %copy-done.5 = f32[3,64]{1,0:T(4,128)S(1)} copy-done((f32[3,64]{1,0:T(4,128)S(1)}, f32[3,64]{1,0:T(4,128)}, u32[]{:S(2)}) %copy-start.5) | copy-done | bytes 792
  5.7 0.0 copy-start.6
  5.7 0.7 %copy-done.6 = f32[4,4]{1,0:T(4,128)S(1)} copy-done((f32[4,4]{1,0:T(4,128)S(1)}, f32[4,4]{1,0:T(4,128)}, u32[]{:S(2)}) %copy-start.6) | copy-done | bytes 88
  6.4 45.3 %shard_map.122 = (f32[64]{0:T(128)S(1)}, f32[3,64]{1,0:T(4,128)S(1)}) custom-call(f32[3,64]{1,0:T(4,128)S(1)} %copy-done.5, s32[64]{0:T(128)S(1)} %copy-done.7, bf16[64,128]{1,0:T(8,128)(2,1)S(1)} %copy-done.3, bf16[128,128]{1,0:T(8,128)(2,1)S(1)} %copy-done, bf16[128,128]{1,0:T(8,128)(2,1)S(1)} %copy-done.1, f32[8,128]{1,0:T(8,128)S(1)} %copy-done.4, ...), custom_call_target="tpu_custom_call" | custom-call | tf_op jit(solution)/shard_map/pallas_call
  51.7 0.5 copy.16
  52.2 0.6 %copy.17 = f32[3,64]{1,0:T(4,128)} copy(f32[3,64]{1,0:T(4,128)S(1)} %get-tuple-element.5) | data formatting | bytes 1536
Async XLA Ops:
  0.6 0.7 %copy-start.9 = (s32[1,4]{1,0:T(1,128)S(1)}, s32[1,4]{1,0:T(1,128)}, u32[]{:S(2)}) copy-start(s32[1,4]{1,0:T(1,128)} %nbr_hbm.1) | copy-start | bytes 52
  0.6 0.7 %copy-start.8 = (f32[128]{0:T(128)S(1)}, f32[128]{0:T(128)}, u32[]{:S(2)}) copy-start(f32[128]{0:T(128)} %readout_hbm.1) | copy-start | bytes 1540
  0.7 0.7 %copy-start.7 = (s32[64]{0:T(128)S(1)}, s32[64]{0:T(128)}, u32[]{:S(2)}) copy-start(s32[64]{0:T(128)} %spc_hbm.1) | copy-start | bytes 772
  1.4 0.8 %copy-start = (bf16[128,128]{1,0:T(8,128)(2,1)S(1)}, bf16[128,128]{1,0:T(8,128)(2,1)}, u32[]{:S(2)}) copy-start(bf16[128,128]{1,0:T(8,128)(2,1)} %wself_hbm.1) | copy-start | bytes 98308
  2.1 0.8 %copy-start.1 = (bf16[128,128]{1,0:T(8,128)(2,1)S(1)}, bf16[128,128]{1,0:T(8,128)(2,1)}, u32[]{:S(2)}) copy-start(bf16[128,128]{1,0:T(8,128)(2,1)} %wsend_hbm.1) | copy-start | bytes 98308
  2.9 0.8 %copy-start.2 = (bf16[128,128]{1,0:T(8,128)(2,1)S(1)}, bf16[128,128]{1,0:T(8,128)(2,1)}, u32[]{:S(2)}) copy-start(bf16[128,128]{1,0:T(8,128)(2,1)} %wmix_hbm.1) | copy-start | bytes 98308
  3.6 0.7 %copy-start.3 = (bf16[64,128]{1,0:T(8,128)(2,1)S(1)}, bf16[64,128]{1,0:T(8,128)(2,1)}, u32[]{:S(2)}) copy-start(bf16[64,128]{1,0:T(8,128)(2,1)} %node_hbm.1) | copy-start | bytes 49156
  4.4 0.7 %copy-start.4 = (f32[8,128]{1,0:T(8,128)S(1)}, f32[8,128]{1,0:T(8,128)}, u32[]{:S(2)}) copy-start(f32[8,128]{1,0:T(8,128)} %radial_hbm.1) | copy-start | bytes 12292
  5.0 0.7 %copy-start.5 = (f32[3,64]{1,0:T(4,128)S(1)}, f32[3,64]{1,0:T(4,128)}, u32[]{:S(2)}) copy-start(f32[3,64]{1,0:T(4,128)} %pos_hbm.1) | copy-start | bytes 2308
  5.7 0.7 %copy-start.6 = (f32[4,4]{1,0:T(4,128)S(1)}, f32[4,4]{1,0:T(4,128)}, u32[]{:S(2)}) copy-start(f32[4,4]{1,0:T(4,128)} %scale_hbm.1) | copy-start | bytes 196

commit v3 on v2

v3 whole, which is shorter than its diff:
```python
import functools

import jax
import jax.numpy as jnp
from jax import lax
from jax.experimental import pallas as pl
from jax.experimental.pallas import tpu as pltpu
from jax.sharding import PartitionSpec as P

BLOCK = 64
C = 128
ROWS = 72
PAIRS = BLOCK * BLOCK
CHUNK = 1024
CENTRES = CHUNK // BLOCK
SPACING = 2.5 / 7
MESH = pl.DeviceIdType.MESH
BF16, F32 = jnp.bfloat16, jnp.float32


def parts(value, count):
    found = []
    for _ in range(count):
        part = value.astype(BF16).astype(F32)
        found.append(part)
        value = value - part
    return found


def dot(left, right):
    return jnp.dot(left, right, preferred_element_type=F32)


def centre_onehot(start, width):
    lane = lax.broadcasted_iota(jnp.int32, (BLOCK, width), 1) + start
    row = lax.broadcasted_iota(jnp.int32, (BLOCK, width), 0)
    return jnp.where((lane // BLOCK) == row, 1.0, 0.0).astype(F32)


def kernel(
    slabs,
    members,
    pos_hbm,
    spc_hbm,
    node_hbm,
    wself_hbm,
    wsend_hbm,
    radial_hbm,
    wmix_hbm,
    readout_hbm,
    scale_hbm,
    nbr_hbm,
    count_hbm,
    energy_ref,
    force_ref,
    pos_ref,
    spc_ref,
    node_ref,
    wself_ref,
    wsend_ref,
    radial_ref,
    wmix_ref,
    readout_ref,
    scale_ref,
    nbr_ref,
    count_ref,
    own,
    asked,
    centres,
    pos_exp,
    scale_exp,
    hot_centre,
    rhs_pair,
    rhs_centre,
    lhs_send,
    lhs_rest,
    lhs_b,
    lhs_r,
    lhs_m,
    ro_exp,
    pair_acc,
    centre_sums,
    grads,
    returned,
    back,
    load_sem,
    ask_send_sem,
    ask_recv_sem,
    own_send_sem,
    own_recv_sem,
    sum_send_sem,
    sum_recv_sem,
    back_send_sem,
    back_recv_sem,
):
    slab, me = lax.axis_index("slab"), lax.axis_index("grp")
    core = lax.rem(slab, 2)
    sib_slab = slab + 1 - 2 * core
    far_slab = lax.rem(slab - 1 + 2 * core + slabs, slabs)

    barrier = pltpu.get_barrier_semaphore()
    partners = [(far_slab, me), (sib_slab, me)]
    mates = [lax.rem(me + k, members) for k in range(1, members)]
    for to in partners + [(slab, mate) for mate in mates]:
        pl.semaphore_signal(barrier, inc=1, device_id=to, device_id_type=MESH)

    loads = [
        pltpu.make_async_copy(source, target, load_sem.at[k])
        for k, (source, target) in enumerate(
            [
                (node_hbm, node_ref),
                (wself_hbm, wself_ref),
                (wsend_hbm, wsend_ref),
                (pos_hbm, pos_ref),
                (spc_hbm, spc_ref),
                (nbr_hbm, nbr_ref),
                (count_hbm, count_ref),
                (radial_hbm, radial_ref),
                (wmix_hbm, wmix_ref),
                (readout_hbm, readout_ref),
                (scale_hbm, scale_ref),
            ]
        )
    ]
    for load in loads:
        load.start()

    def spread_hot(step, carry):
        lanes = pl.ds(pl.multiple_of(step * CHUNK, CHUNK), CHUNK)
        hot_centre[:, lanes] = centre_onehot(step * CHUNK, CHUNK).astype(BF16)
        return carry

    for load in loads[:7]:
        load.wait()

    species = spc_ref[...].astype(F32).reshape(1, BLOCK)
    pad = jnp.zeros((1, BLOCK), F32)
    place = jnp.concatenate([pos_ref[...], species, pad, pad, pad, pad], axis=0)
    place = jnp.concatenate([place, jnp.zeros_like(place)], axis=1)
    features = dot(node_ref[...], wself_ref[...])
    own[me, 0:BLOCK, :] = dot(node_ref[...], wsend_ref[...])
    own[me, BLOCK:ROWS, :] = place
    asked_row = lax.broadcasted_iota(jnp.int32, (3 * members, C), 0)

    def slots_in(panel, first):
        hot = jnp.zeros((3 * members, C), F32)
        for k, slot in enumerate((first, 2, 3)):
            other = nbr_ref[0, slot]
            wanted = jnp.where(
                (other // members == panel) & (slot < count_ref[0]),
                lax.rem(other, members) + k * members,
                -1,
            )
            hot = jnp.where(asked_row == wanted, 1.0, hot)
        return hot

    for k, (panel, first) in enumerate(((2 * core, core), (2 - 2 * core, 1 - core))):
        centres[k, 0:BLOCK, :] = features
        centres[k, BLOCK:ROWS, :] = place
        centres[k, ROWS:, :] = slots_in(panel, first)
    asked[2, 0:BLOCK, :] = features
    asked[2, BLOCK:ROWS, :] = place
    asked[2, ROWS:, :] = slots_in(1, 2)

    pl.semaphore_wait(barrier, members + 1)

    def ask(k):
        return pltpu.make_async_remote_copy(
            src_ref=centres.at[k],
            dst_ref=asked.at[k],
            send_sem=ask_send_sem.at[k],
            recv_sem=ask_recv_sem.at[k],
            device_id=partners[k],
            device_id_type=MESH,
        )

    ask(0).start()
    for mate in mates:
        pltpu.make_async_remote_copy(
            src_ref=own.at[me],
            dst_ref=own.at[me],
            send_sem=own_send_sem,
            recv_sem=own_recv_sem,
            device_id=(slab, mate),
            device_id_type=MESH,
        ).start()
    ask(1).start()

    lax.fori_loop(0, PAIRS // CHUNK, spread_hot, 0)
    atom = lax.broadcasted_iota(jnp.int32, (BLOCK, CHUNK), 0)
    lane = lax.broadcasted_iota(jnp.int32, (BLOCK, CHUNK), 1)
    hot_j = jnp.where(lax.rem(lane, BLOCK) == atom, 1.0, 0.0).astype(F32)
    rhs_pair[...] = jnp.concatenate([hot_j, hot_j], axis=0).astype(BF16)
    hot_i = centre_onehot(0, CHUNK)[0:CENTRES]
    rhs_centre[...] = jnp.concatenate([hot_i, hot_i], axis=0).astype(BF16)
    for load in loads[7:]:
        load.wait()
    radial_hi, radial_lo = parts(radial_ref[...], 2)
    lhs_r[...] = (jnp.concatenate([radial_hi, radial_lo], axis=0) * 0.25).astype(BF16)
    lhs_m[...] = (wmix_ref[...].astype(F32).T * 0.5).astype(BF16)
    ones = jnp.ones((16, C), F32)
    lhs_b[...] = jnp.concatenate(
        [
            jnp.concatenate([jnp.zeros((C, C), F32), ones], axis=0),
            jnp.concatenate([wmix_ref[...].astype(F32), jnp.zeros((16, C), F32)], axis=0),
        ],
        axis=1,
    ).astype(BF16)
    readout = readout_ref[...].reshape(1, C)
    ro_exp[...] = jnp.broadcast_to(readout, (C, C)).T
    grads[...] = jnp.zeros_like(grads)

    row8 = lax.broadcasted_iota(jnp.int32, (8, BLOCK), 0)
    row = lax.broadcasted_iota(jnp.int32, (8, CHUNK), 0)
    pair = lax.broadcasted_iota(jnp.int32, (1, CHUNK), 1)
    center = row.astype(F32) * SPACING
    gap = lax.rem(pair, BLOCK) - pair // BLOCK
    mates_blocks = own.at[pl.ds(0, members - 1)]
    mates_grads = grads.at[pl.ds(0, members - 1)]

    def group(turn, carry):
        which = jnp.where(slab < 2, 2 - turn, turn)

        @pl.when(turn == 0)
        def _():
            pltpu.make_async_copy(mates_blocks, mates_blocks, own_recv_sem).wait()

        @pl.when(which == 0)
        def _():
            ask(0).wait_recv()

        @pl.when(which == 1)
        def _():
            ask(1).wait_recv()

        spot = asked[which, BLOCK:ROWS, 0:BLOCK]
        scale8 = jnp.zeros((8, BLOCK), F32)
        for r in range(4):
            for s in range(4):
                there = (row8 == s) & (spot[3:4] == float(r))
                scale8 = jnp.where(there, scale_ref[r, s], scale8)
        small = jnp.concatenate(parts(spot, 3) + parts(scale8, 3), axis=0).astype(BF16)
        half_hi, half_lo = parts(radial_ref[...] * 0.5, 2)
        for k in range(PAIRS // CHUNK):
            mine = pl.ds(k * CENTRES, CENTRES)
            self_hi, self_lo = parts(asked[which, mine, :] * 0.5, 2)
            rest = [half_hi, half_lo, half_hi, jnp.zeros((8, C), F32), self_hi, self_lo]
            lhs_rest[k] = jnp.concatenate(rest, axis=0).T.astype(BF16)
            lanes = slice(k * CHUNK, (k + 1) * CHUNK)
            spread = dot(small, hot_centre[:, lanes])
            pos_exp[:, lanes] = spread[0:8] + spread[8:16] + spread[16:24]
            scale_exp[:, lanes] = spread[24:32] + spread[32:40] + spread[40:48]
        pair_acc[...] = jnp.zeros_like(pair_acc)

        def tile(slot, carry):
            hot = asked[which, pl.ds(pl.multiple_of(ROWS + slot * members, 8), members), :]
            block = own[0] * hot[0:1]
            for k in range(1, members):
                block = block + own[k] * hot[k : k + 1]
            live = jnp.concatenate([jnp.sum(hot, axis=0, keepdims=True)] * (CHUNK // C), axis=1)
            self_hot = asked[which, pl.ds(ROWS + slot * members + me, 1), :]
            self_hot = jnp.where(which == 2, self_hot, 0.0)
            self_hot = jnp.concatenate([self_hot] * (CHUNK // C), axis=1)
            place_j = jnp.concatenate([block[BLOCK:ROWS, 0:BLOCK]] * (CHUNK // BLOCK), axis=1)
            kind_hot = jnp.where(place_j[3:4] == row.astype(F32), 1.0, 0.0)
            lhs_send[...] = jnp.concatenate(parts(block[0:BLOCK] * 0.5, 2), axis=0).T.astype(BF16)

            def first(turn):
                lanes = slice(turn * CHUNK, (turn + 1) * CHUNK)
                diff = jnp.where(row < 3, place_j - pos_exp[:, lanes], 0.0)
                dist_sq = jnp.sum(diff * diff, axis=0, keepdims=True)
                scale = jnp.sum(scale_exp[:, lanes] * kind_hot, axis=0, keepdims=True)
                scaled = dist_sq * scale
                keep = live - jnp.where(gap == turn * CENTRES, self_hot, 0.0)
                reach = jnp.maximum(1.0 - scaled * (1.0 / 2.5), 0.0)
                offset = (scaled - center) * (1.0 / SPACING)
                basis = jnp.exp(-(offset * offset))
                slope = basis * offset * (-2.0 / SPACING)
                basis_hi, basis_lo = parts(basis, 2)
                head = jnp.concatenate(
                    [basis_hi, basis_hi, basis_lo, jnp.zeros((8, CHUNK), F32)], axis=0
                ).astype(BF16)
                rhs = jnp.concatenate([rhs_pair[...], head, rhs_centre[...]], axis=0)
                lhs = jnp.concatenate([lhs_send[...], lhs_rest[turn]], axis=1)
                return lanes, diff, scale, keep, reach, slope, dot(lhs, rhs)

            def second(state):
                half = state[-1]
                t = jnp.tanh(half)
                p = 1.0 + t
                hidden = half * p
                slope_1 = p + hidden * (1.0 - t)
                half = dot(lhs_m[...], hidden.astype(BF16))
                return state[:-1] + (slope_1, half)

            def third(state):
                half = state[-1]
                t = jnp.tanh(half)
                p = (1.0 + t) * jnp.concatenate([ro_exp[...]] * (CHUNK // C), axis=1)
                mixed = half * p
                slope_2 = p + mixed * (1.0 - t)
                out = dot(lhs_b[...], jnp.concatenate([mixed, slope_2], axis=0).astype(BF16))
                return state[:-1] + (out,)

            def fourth(state):
                lanes, diff, scale, keep, reach, slope, slope_1, out = state
                d_basis = dot(lhs_r[...], (out[0:C] * slope_1).astype(BF16))
                d_basis = d_basis[0:8] + d_basis[8:16]
                energy = out[C : C + 1]
                cut = reach * reach
                d_scaled = cut * jnp.sum(d_basis * slope, axis=0, keepdims=True)
                d_scaled = d_scaled - (2.0 / 2.5) * reach * energy
                force = (2.0 * keep * scale * d_scaled) * diff
                found = jnp.where(row == 3, keep * cut * energy, force)
                pair_acc[:, lanes] += found
                total = found[:, 0:C]
                for k in range(1, CHUNK // C):
                    total = total + found[:, k * C : (k + 1) * C]
                return total

            stages = [first, second, third, fourth]
            states = {}
            total = None
            count = PAIRS // CHUNK
            for turn in range(count + 3):
                for depth in range(4):
                    sub = turn - depth
                    if 0 <= sub < count:
                        states[sub] = stages[depth](states.get(sub, sub))
                        if depth == 3:
                            part = states.pop(sub)
                            total = part if total is None else total + part
            grad = total[:, 0:BLOCK] + total[:, BLOCK:C]
            grad = jnp.concatenate([grad, jnp.zeros_like(grad)], axis=1)
            for k in range(members):
                grads[k] += grad * hot[k : k + 1]
            return carry

        lax.fori_loop(jnp.where(which == 2, 1, 0), 3, tile, 0)

        total = jnp.zeros((24, BLOCK), F32)
        for k in range(PAIRS // CHUNK):
            lanes = slice(k * CHUNK, (k + 1) * CHUNK)
            split = jnp.concatenate(parts(pair_acc[:, lanes], 3), axis=0).astype(BF16)
            total = total + lax.dot_general(
                split,
                hot_centre[:, lanes],
                (((1,), (1,)), ((), ())),
                preferred_element_type=F32,
            )
        total = total[0:8] + total[8:16] + total[16:24]
        centre_sums[which] = jnp.concatenate([total, jnp.zeros_like(total)], axis=1)

        @pl.when(which == 0)
        def _():
            tell(0).start()

        @pl.when(which == 1)
        def _():
            tell(1).start()

        return carry

    def tell(k):
        return pltpu.make_async_remote_copy(
            src_ref=centre_sums.at[k],
            dst_ref=returned.at[k],
            send_sem=sum_send_sem.at[k],
            recv_sem=sum_recv_sem.at[k],
            device_id=partners[k],
            device_id_type=MESH,
        )

    lax.fori_loop(0, 3, group, 0)

    for mate in mates:
        pltpu.make_async_remote_copy(
            src_ref=grads.at[mate],
            dst_ref=back.at[me],
            send_sem=back_send_sem,
            recv_sem=back_recv_sem,
            device_id=(slab, mate),
            device_id_type=MESH,
        ).start()
    back[me] = grads[me]

    tell(0).wait_recv()
    tell(1).wait_recv()
    centre_sum = centre_sums[2] + returned[0] + returned[1]
    energy_ref[...] = centre_sum[3:4, 0:BLOCK].reshape(BLOCK)
    pltpu.make_async_copy(mates_grads, mates_grads, back_recv_sem).wait()
    total = back[0]
    for k in range(1, members):
        total = total + back[k]
    force_ref[...] = (centre_sum - total)[0:3, 0:BLOCK]

    for k in range(2):
        ask(k).wait_send()
        tell(k).wait_send()
    pltpu.make_async_copy(mates_blocks, mates_blocks, own_send_sem).wait()
    pltpu.make_async_copy(mates_grads, mates_grads, back_send_sem).wait()


def solution(mesh):
    slabs, members = mesh.shape["slab"], mesh.shape["grp"]
    vmem = pl.BlockSpec(memory_space=pltpu.VMEM)
    call = pl.pallas_call(
        functools.partial(kernel, slabs, members),
        out_shape=(
            jax.ShapeDtypeStruct((BLOCK,), F32),
            jax.ShapeDtypeStruct((3, BLOCK), F32),
        ),
        in_specs=[pl.BlockSpec(memory_space=pltpu.HBM)] * 11,
        out_specs=(vmem, vmem),
        scratch_shapes=[
            pltpu.VMEM((3, BLOCK), F32),
            pltpu.VMEM((BLOCK,), jnp.int32),
            pltpu.VMEM((BLOCK, C), BF16),
            pltpu.VMEM((C, C), BF16),
            pltpu.VMEM((C, C), BF16),
            pltpu.VMEM((8, C), F32),
            pltpu.VMEM((C, C), BF16),
            pltpu.VMEM((C,), F32),
            pltpu.SMEM((4, 4), F32),
            pltpu.SMEM((1, 4), jnp.int32),
            pltpu.SMEM((1,), jnp.int32),
            pltpu.VMEM((members, ROWS, C), F32),
            pltpu.VMEM((3, ROWS + 3 * members, C), F32),
            pltpu.VMEM((2, ROWS + 3 * members, C), F32),
            pltpu.VMEM((8, PAIRS), F32),
            pltpu.VMEM((8, PAIRS), F32),
            pltpu.VMEM((BLOCK, PAIRS), BF16),
            pltpu.VMEM((2 * BLOCK, CHUNK), BF16),
            pltpu.VMEM((2 * CENTRES, CHUNK), BF16),
            pltpu.VMEM((C, 2 * BLOCK), BF16),
            pltpu.VMEM((PAIRS // CHUNK, C, 32 + 2 * CENTRES), BF16),
            pltpu.VMEM((C + 16, 2 * C), BF16),
            pltpu.VMEM((16, C), BF16),
            pltpu.VMEM((C, C), BF16),
            pltpu.VMEM((C, C), F32),
            pltpu.VMEM((8, PAIRS), F32),
            pltpu.VMEM((3, 8, C), F32),
            pltpu.VMEM((members, 8, C), F32),
            pltpu.VMEM((2, 8, C), F32),
            pltpu.VMEM((members, 8, C), F32),
            pltpu.SemaphoreType.DMA((11,)),
            pltpu.SemaphoreType.DMA((2,)),
            pltpu.SemaphoreType.DMA((2,)),
            pltpu.SemaphoreType.DMA,
            pltpu.SemaphoreType.DMA,
            pltpu.SemaphoreType.DMA((2,)),
            pltpu.SemaphoreType.DMA((2,)),
            pltpu.SemaphoreType.DMA,
            pltpu.SemaphoreType.DMA,
        ],
        compiler_params=pltpu.CompilerParams(
            collective_id=0, has_side_effects=True, vmem_limit_bytes=60 * 2**20
        ),
    )
    return jax.shard_map(
        call,
        mesh=mesh,
        in_specs=(
            P(None, ("slab", "grp")),
            P(("slab", "grp")),
            P(("slab", "grp"), None),
            P(),
            P(),
            P(),
            P(),
            P(),
            P(),
            P(("slab", "grp"), None),
            P(("slab", "grp")),
        ),
        out_specs=(P(("slab", "grp")), P(None, ("slab", "grp"))),
        check_vma=False,
    )
```

time: 53.3 us -> 49.2 us (0.923)
  the two profiles are of different devices: /device:TPU:8 before, /device:TPU:6 now
where the time goes in v3:
time: 49.2 us; the launch traced here: 48.9 us
  Pallas kernels  45.9 us (93%)
  local copies, waits for them, and re-layouts  1.71 us (3%)
  between operations  1.31 us (3%)
    pallas_call x1, Pallas kernels  45.9 us
    unnamed x6, local copies, waits for them, and re-layouts  1.71 us

profile of v3, /device:TPU:6, one launch (start us, length us, event | category | flops | bytes accessed | tf_op | source)
XLA Modules:
  0.0 48.9 jit_solution(3820282059528190534)
XLA Ops:
  1.3 45.9 %shard_map.122 = (f32[64]{0:T(128)}, f32[3,64]{1,0:T(4,128)}) custom-call(f32[3,64]{1,0:T(4,128)} %pos_hbm.1, s32[64]{0:T(128)} %spc_hbm.1, bf16[64,128]{1,0:T(8,128)(2,1)} %node_hbm.1, bf16[128,128]{1,0:T(8,128)(2,1)} %wself_hbm.1, bf16[128,128]{1,0:T(8,128)(2,1)} %wsend_hbm.1, f32[8,128]{1,0:T(8,128)} %radial_hbm.1, bf16[128,128]{1,0:T(8,128)(2,1)} %wmix_hbm.1, ...), custom_call_target="tpu_custom_call" | custom-call | tf_op jit(solution)/shard_map/pallas_call
  47.2 0.0 copy-start.1
  47.2 0.0 copy-start
  47.2 0.6 %copy-done.1 = f32[64]{0:T(128)S(1)} copy-done((f32[64]{0:T(128)S(1)}, f32[64]{0:T(128)}, u32[]{:S(2)}) %copy-start.1) | copy-done | bytes 280
  47.9 0.5 %copy.16 = f32[64]{0:T(128)} copy(f32[64]{0:T(128)S(1)} %copy-done.1) | data formatting | bytes 512
  48.4 0.0 copy-done
  48.4 0.6 %copy.17 = f32[3,64]{1,0:T(4,128)} copy(f32[3,64]{1,0:T(4,128)S(1)} %copy-done) | data formatting | bytes 1536
Async XLA Ops:
  47.2 0.6 %copy-start.1 = (f32[64]{0:T(128)S(1)}, f32[64]{0:T(128)}, u32[]{:S(2)}) copy-start(f32[64]{0:T(128)} %get-tuple-element.4) | copy-start | bytes 772
  47.2 1.1 %copy-start = (f32[3,64]{1,0:T(4,128)S(1)}, f32[3,64]{1,0:T(4,128)}, u32[]{:S(2)}) copy-start(f32[3,64]{1,0:T(4,128)} %get-tuple-element.5) | copy-start | bytes 2308

commit v4 on v3

--- a/solution.py
+++ b/solution.py
@@ -65,8 +65,10 @@
     nbr_ref,
     count_ref,
     own,
+    near,
     asked,
     centres,
+    block_ref,
     pos_exp,
     scale_exp,
     hot_centre,
@@ -81,17 +83,19 @@
     pair_acc,
     centre_sums,
     grads,
+    near_grads,
+    near_back,
     returned,
     back,
     load_sem,
-    ask_send_sem,
-    ask_recv_sem,
+    send_sem,
+    recv_sem,
     own_send_sem,
     own_recv_sem,
-    sum_send_sem,
-    sum_recv_sem,
     back_send_sem,
     back_recv_sem,
+    group_sem,
+    far_sem,
 ):
     slab, me = lax.axis_index("slab"), lax.axis_index("grp")
     core = lax.rem(slab, 2)
@@ -99,10 +103,15 @@
     far_slab = lax.rem(slab - 1 + 2 * core + slabs, slabs)
 
     barrier = pltpu.get_barrier_semaphore()
-    partners = [(far_slab, me), (sib_slab, me)]
     mates = [lax.rem(me + k, members) for k in range(1, members)]
-    for to in partners + [(slab, mate) for mate in mates]:
-        pl.semaphore_signal(barrier, inc=1, device_id=to, device_id_type=MESH)
+    far_hub = lax.rem(slab + jnp.where(core == 0, slabs - 1, 2), slabs)
+    pl.semaphore_signal(barrier, inc=1, device_id=(far_hub, me), device_id_type=MESH)
+    for mate in mates:
+        pl.semaphore_signal(barrier, inc=1, device_id=(slab - core, mate), device_id_type=MESH)
+
+    @pl.when(core == 1)
+    def _():
+        pl.semaphore_signal(barrier, inc=1, device_id=(sib_slab, me), device_id_type=MESH)
 
     loads = [
         pltpu.make_async_copy(source, target, load_sem.at[k])
@@ -154,27 +163,23 @@
             hot = jnp.where(asked_row == wanted, 1.0, hot)
         return hot
 
-    for k, (panel, first) in enumerate(((2 * core, core), (2 - 2 * core, 1 - core))):
-        centres[k, 0:BLOCK, :] = features
-        centres[k, BLOCK:ROWS, :] = place
-        centres[k, ROWS:, :] = slots_in(panel, first)
-    asked[2, 0:BLOCK, :] = features
-    asked[2, BLOCK:ROWS, :] = place
-    asked[2, ROWS:, :] = slots_in(1, 2)
-
-    pl.semaphore_wait(barrier, members + 1)
-
-    def ask(k):
-        return pltpu.make_async_remote_copy(
-            src_ref=centres.at[k],
-            dst_ref=asked.at[k],
-            send_sem=ask_send_sem.at[k],
-            recv_sem=ask_recv_sem.at[k],
-            device_id=partners[k],
-            device_id_type=MESH,
-        )
-
-    ask(0).start()
+    centres[0:BLOCK, :] = features
+    centres[BLOCK:ROWS, :] = place
+    centres[ROWS:, :] = slots_in(2 * core, core)
+    asked[1, 0:BLOCK, :] = features
+    asked[1, BLOCK:ROWS, :] = place
+    asked[1, ROWS : ROWS + 3 * members, :] = slots_in(1, 1 - core)
+    asked[1, ROWS + 3 * members :, :] = slots_in(2 - 2 * core, 1 - core)
+
+    @pl.when(core == 0)
+    def _():
+        pl.semaphore_wait(barrier, 2 * members - 1)
+        pl.semaphore_signal(group_sem, inc=1, device_id=(sib_slab, me), device_id_type=MESH)
+
+    @pl.when(core == 1)
+    def _():
+        pl.semaphore_wait(group_sem, 1)
+
     for mate in mates:
         pltpu.make_async_remote_copy(
             src_ref=own.at[me],
@@ -184,7 +189,36 @@
             device_id=(slab, mate),
             device_id_type=MESH,
         ).start()
-    ask(1).start()
+
+    def copy(index, source, target, to_slab):
+        return pltpu.make_async_remote_copy(
+            src_ref=source,
+            dst_ref=target,
+            send_sem=send_sem.at[index],
+            recv_sem=recv_sem.at[index],
+            device_id=(to_slab, me),
+            device_id_type=MESH,
+        )
+
+    ask = copy(0, centres, asked.at[0, pl.ds(0, ROWS + 3 * members)], far_slab)
+    tell = copy(1, centre_sums.at[0], returned, far_slab)
+    lend = copy(2, own, near, sib_slab)
+    repay = copy(3, near_grads, near_back, sib_slab)
+    early = slab < 2
+
+    def ask_far():
+        @pl.when(core == 0)
+        def _():
+            pl.semaphore_wait(far_sem, 1)
+
+        @pl.when(core == 1)
+        def _():
+            pl.semaphore_wait(barrier, 2)
+            pl.semaphore_signal(far_sem, inc=1, device_id=(sib_slab, me), device_id_type=MESH)
+
+        ask.start()
+
+    pl.when(jnp.logical_not(early))(ask_far)
 
     lax.fori_loop(0, PAIRS // CHUNK, spread_hot, 0)
     atom = lax.broadcasted_iota(jnp.int32, (BLOCK, CHUNK), 0)
@@ -209,6 +243,7 @@
     readout = readout_ref[...].reshape(1, C)
     ro_exp[...] = jnp.broadcast_to(readout, (C, C)).T
     grads[...] = jnp.zeros_like(grads)
+    near_grads[...] = jnp.zeros_like(near_grads)
 
     row8 = lax.broadcasted_iota(jnp.int32, (8, BLOCK), 0)
     row = lax.broadcasted_iota(jnp.int32, (8, CHUNK), 0)
@@ -218,20 +253,19 @@
     mates_blocks = own.at[pl.ds(0, members - 1)]
     mates_grads = grads.at[pl.ds(0, members - 1)]
 
+    pltpu.make_async_copy(mates_blocks, mates_blocks, own_recv_sem).wait()
+    lend.start()
+
     def group(turn, carry):
-        which = jnp.where(slab < 2, 2 - turn, turn)
-
-        @pl.when(turn == 0)
-        def _():
-            pltpu.make_async_copy(mates_blocks, mates_blocks, own_recv_sem).wait()
+        which = jnp.where(early, 1 - turn, turn)
 
         @pl.when(which == 0)
         def _():
-            ask(0).wait_recv()
+            ask.wait_recv()
 
         @pl.when(which == 1)
         def _():
-            ask(1).wait_recv()
+            lend.wait_recv()
 
         spot = asked[which, BLOCK:ROWS, 0:BLOCK]
         scale8 = jnp.zeros((8, BLOCK), F32)
@@ -253,14 +287,35 @@
         pair_acc[...] = jnp.zeros_like(pair_acc)
 
         def tile(slot, carry):
-            hot = asked[which, pl.ds(pl.multiple_of(ROWS + slot * members, 8), members), :]
-            block = own[0] * hot[0:1]
+            @pl.when(early & (which == 1) & (slot == 1))
+            def _():
+                ask_far()
+
+            hot_rows = pl.ds(pl.multiple_of(ROWS + slot * members, 8), members)
+            near_rows = pl.ds(pl.multiple_of(ROWS + (slot + 3) * members, 8), members)
+            hot = asked[which, hot_rows, :]
+            live = jnp.sum(hot, axis=0, keepdims=True)
+            self_hot = asked[which, pl.ds(ROWS + slot * members + me, 1), :]
+            self_hot = jnp.where(which == 1, self_hot, 0.0)
+            self_hot = jnp.concatenate([self_hot] * (CHUNK // C), axis=1)
+            chosen = own[0] * hot[0:1]
             for k in range(1, members):
-                block = block + own[k] * hot[k : k + 1]
-            live = jnp.concatenate([jnp.sum(hot, axis=0, keepdims=True)] * (CHUNK // C), axis=1)
-            self_hot = asked[which, pl.ds(ROWS + slot * members + me, 1), :]
-            self_hot = jnp.where(which == 2, self_hot, 0.0)
-            self_hot = jnp.concatenate([self_hot] * (CHUNK // C), axis=1)
+                chosen = chosen + own[k] * hot[k : k + 1]
+            block_ref[0:ROWS, :] = chosen
+            block_ref[ROWS:, :] = jnp.broadcast_to(live, (8, C))
+
+            @pl.when(which == 1)
+            def _():
+                near_hot = asked[which, near_rows, :]
+                chosen = block_ref[0:ROWS, :]
+                for k in range(members):
+                    chosen = chosen + near[k] * near_hot[k : k + 1]
+                block_ref[0:ROWS, :] = chosen
+                near_live = jnp.sum(near_hot, axis=0, keepdims=True)
+                block_ref[ROWS:, :] += jnp.broadcast_to(near_live, (8, C))
+
+            block = block_ref[0:ROWS, :]
+            live = jnp.concatenate([block_ref[ROWS : ROWS + 1, :]] * (CHUNK // C), axis=1)
             place_j = jnp.concatenate([block[BLOCK:ROWS, 0:BLOCK]] * (CHUNK // BLOCK), axis=1)
             kind_hot = jnp.where(place_j[3:4] == row.astype(F32), 1.0, 0.0)
             lhs_send[...] = jnp.concatenate(parts(block[0:BLOCK] * 0.5, 2), axis=0).T.astype(BF16)
@@ -334,9 +389,16 @@
             grad = jnp.concatenate([grad, jnp.zeros_like(grad)], axis=1)
             for k in range(members):
                 grads[k] += grad * hot[k : k + 1]
+
+            @pl.when(which == 1)
+            def _():
+                near_hot = asked[which, near_rows, :]
+                for k in range(members):
+                    near_grads[k] += grad * near_hot[k : k + 1]
+
             return carry
 
-        lax.fori_loop(jnp.where(which == 2, 1, 0), 3, tile, 0)
+        lax.fori_loop(0, 3, tile, 0)
 
         total = jnp.zeros((24, BLOCK), F32)
         for k in range(PAIRS // CHUNK):
@@ -353,26 +415,18 @@
 
         @pl.when(which == 0)
         def _():
-            tell(0).start()
+            tell.start()
 
         @pl.when(which == 1)
         def _():
-            tell(1).start()
+            repay.start()
 
         return carry
 
-    def tell(k):
-        return pltpu.make_async_remote_copy(
-            src_ref=centre_sums.at[k],
-            dst_ref=returned.at[k],
-            send_sem=sum_send_sem.at[k],
-            recv_sem=sum_recv_sem.at[k],
-            device_id=partners[k],
-            device_id_type=MESH,
-        )
-
-    lax.fori_loop(0, 3, group, 0)
-
+    lax.fori_loop(0, 2, group, 0)
+
+    repay.wait_recv()
+    grads[...] += near_back[...]
     for mate in mates:
         pltpu.make_async_remote_copy(
             src_ref=grads.at[mate],
@@ -384,9 +438,8 @@
         ).start()
     back[me] = grads[me]
 
-    tell(0).wait_recv()
-    tell(1).wait_recv()
-    centre_sum = centre_sums[2] + returned[0] + returned[1]
+    tell.wait_recv()
+    centre_sum = centre_sums[1] + returned[...]
     energy_ref[...] = centre_sum[3:4, 0:BLOCK].reshape(BLOCK)
     pltpu.make_async_copy(mates_grads, mates_grads, back_recv_sem).wait()
     total = back[0]
@@ -394,9 +447,8 @@
         total = total + back[k]
     force_ref[...] = (centre_sum - total)[0:3, 0:BLOCK]
 
-    for k in range(2):
-        ask(k).wait_send()
-        tell(k).wait_send()
+    for sent in (ask, tell, lend, repay):
+        sent.wait_send()
     pltpu.make_async_copy(mates_blocks, mates_blocks, own_send_sem).wait()
     pltpu.make_async_copy(mates_grads, mates_grads, back_send_sem).wait()
 
@@ -425,8 +477,10 @@
             pltpu.SMEM((1, 4), jnp.int32),
             pltpu.SMEM((1,), jnp.int32),
             pltpu.VMEM((members, ROWS, C), F32),
-            pltpu.VMEM((3, ROWS + 3 * members, C), F32),
-            pltpu.VMEM((2, ROWS + 3 * members, C), F32),
+            pltpu.VMEM((members, ROWS, C), F32),
+            pltpu.VMEM((2, ROWS + 6 * members, C), F32),
+            pltpu.VMEM((ROWS + 3 * members, C), F32),
+            pltpu.VMEM((ROWS + 8, C), F32),
             pltpu.VMEM((8, PAIRS), F32),
             pltpu.VMEM((8, PAIRS), F32),
             pltpu.VMEM((BLOCK, PAIRS), BF16),
@@ -439,19 +493,21 @@
             pltpu.VMEM((C, C), BF16),
             pltpu.VMEM((C, C), F32),
             pltpu.VMEM((8, PAIRS), F32),
-            pltpu.VMEM((3, 8, C), F32),
-            pltpu.VMEM((members, 8, C), F32),
             pltpu.VMEM((2, 8, C), F32),
             pltpu.VMEM((members, 8, C), F32),
+            pltpu.VMEM((members, 8, C), F32),
+            pltpu.VMEM((members, 8, C), F32),
+            pltpu.VMEM((8, C), F32),
+            pltpu.VMEM((members, 8, C), F32),
             pltpu.SemaphoreType.DMA((11,)),
-            pltpu.SemaphoreType.DMA((2,)),
-            pltpu.SemaphoreType.DMA((2,)),
+            pltpu.SemaphoreType.DMA((4,)),
+            pltpu.SemaphoreType.DMA((4,)),
             pltpu.SemaphoreType.DMA,
             pltpu.SemaphoreType.DMA,
-            pltpu.SemaphoreType.DMA((2,)),
-            pltpu.SemaphoreType.DMA((2,)),
             pltpu.SemaphoreType.DMA,
             pltpu.SemaphoreType.DMA,
+            pltpu.SemaphoreType.REGULAR,
+            pltpu.SemaphoreType.REGULAR,
         ],
         compiler_params=pltpu.CompilerParams(
             collective_id=0, has_side_effects=True, vmem_limit_bytes=60 * 2**20

time: 49.2 us -> 46.9 us (0.953)
  the two profiles are of different devices: /device:TPU:6 before, /device:TPU:17 now
where the time goes in v4:
time: 46.9 us; the launch traced here: 46.6 us
  Pallas kernels  43.6 us (93%)
  local copies, waits for them, and re-layouts  1.71 us (4%)
  between operations  1.31 us (3%)
    pallas_call x1, Pallas kernels  43.6 us
    unnamed x6, local copies, waits for them, and re-layouts  1.71 us

profile of v4, /device:TPU:17, one launch (start us, length us, event | category | flops | bytes accessed | tf_op | source)
XLA Modules:
  0.0 46.6 jit_solution(3053123562807966020)
XLA Ops:
  1.3 43.6 %shard_map.122 = (f32[64]{0:T(128)}, f32[3,64]{1,0:T(4,128)}) custom-call(f32[3,64]{1,0:T(4,128)} %pos_hbm.1, s32[64]{0:T(128)} %spc_hbm.1, bf16[64,128]{1,0:T(8,128)(2,1)} %node_hbm.1, bf16[128,128]{1,0:T(8,128)(2,1)} %wself_hbm.1, bf16[128,128]{1,0:T(8,128)(2,1)} %wsend_hbm.1, f32[8,128]{1,0:T(8,128)} %radial_hbm.1, bf16[128,128]{1,0:T(8,128)(2,1)} %wmix_hbm.1, ...), custom_call_target="tpu_custom_call" | custom-call | tf_op jit(solution)/shard_map/pallas_call
  44.9 0.0 copy-start.1
  44.9 0.0 copy-start
  44.9 0.6 %copy-done.1 = f32[64]{0:T(128)S(1)} copy-done((f32[64]{0:T(128)S(1)}, f32[64]{0:T(128)}, u32[]{:S(2)}) %copy-start.1) | copy-done | bytes 280
  45.5 0.5 %copy.16 = f32[64]{0:T(128)} copy(f32[64]{0:T(128)S(1)} %copy-done.1) | data formatting | bytes 512
  46.0 0.0 copy-done
  46.1 0.6 %copy.17 = f32[3,64]{1,0:T(4,128)} copy(f32[3,64]{1,0:T(4,128)S(1)} %copy-done) | data formatting | bytes 1536
Async XLA Ops:
  44.9 0.6 %copy-start.1 = (f32[64]{0:T(128)S(1)}, f32[64]{0:T(128)}, u32[]{:S(2)}) copy-start(f32[64]{0:T(128)} %get-tuple-element.4) | copy-start | bytes 772
  44.9 1.1 %copy-start = (f32[3,64]{1,0:T(4,128)S(1)}, f32[3,64]{1,0:T(4,128)}, u32[]{:S(2)}) copy-start(f32[3,64]{1,0:T(4,128)} %get-tuple-element.5) | copy-start | bytes 2308

commit v5 on v4

--- a/solution.py
+++ b/solution.py
@@ -95,7 +95,6 @@
     back_send_sem,
     back_recv_sem,
     group_sem,
-    far_sem,
 ):
     slab, me = lax.axis_index("slab"), lax.axis_index("grp")
     core = lax.rem(slab, 2)
@@ -104,12 +103,13 @@
 
     barrier = pltpu.get_barrier_semaphore()
     mates = [lax.rem(me + k, members) for k in range(1, members)]
-    far_hub = lax.rem(slab + jnp.where(core == 0, slabs - 1, 2), slabs)
-    pl.semaphore_signal(barrier, inc=1, device_id=(far_hub, me), device_id_type=MESH)
+    pl.semaphore_signal(barrier, inc=1, device_id=(far_slab, me), device_id_type=MESH)
     for mate in mates:
-        pl.semaphore_signal(barrier, inc=1, device_id=(slab - core, mate), device_id_type=MESH)
-
-    @pl.when(core == 1)
+        pl.semaphore_signal(
+            barrier, inc=1, device_id=(slab + 1 - core, mate), device_id_type=MESH
+        )
+
+    @pl.when(core == 0)
     def _():
         pl.semaphore_signal(barrier, inc=1, device_id=(sib_slab, me), device_id_type=MESH)
 
@@ -171,12 +171,12 @@
     asked[1, ROWS : ROWS + 3 * members, :] = slots_in(1, 1 - core)
     asked[1, ROWS + 3 * members :, :] = slots_in(2 - 2 * core, 1 - core)
 
+    @pl.when(core == 1)
+    def _():
+        pl.semaphore_wait(barrier, 2 * members)
+        pl.semaphore_signal(group_sem, inc=1, device_id=(sib_slab, me), device_id_type=MESH)
+
     @pl.when(core == 0)
-    def _():
-        pl.semaphore_wait(barrier, 2 * members - 1)
-        pl.semaphore_signal(group_sem, inc=1, device_id=(sib_slab, me), device_id_type=MESH)
-
-    @pl.when(core == 1)
     def _():
         pl.semaphore_wait(group_sem, 1)
 
@@ -204,17 +204,12 @@
     tell = copy(1, centre_sums.at[0], returned, far_slab)
     lend = copy(2, own, near, sib_slab)
     repay = copy(3, near_grads, near_back, sib_slab)
-    early = slab < 2
+    early = slab == 0
 
     def ask_far():
         @pl.when(core == 0)
         def _():
-            pl.semaphore_wait(far_sem, 1)
-
-        @pl.when(core == 1)
-        def _():
-            pl.semaphore_wait(barrier, 2)
-            pl.semaphore_signal(far_sem, inc=1, device_id=(sib_slab, me), device_id_type=MESH)
+            pl.semaphore_wait(barrier, 1)
 
         ask.start()
 
@@ -507,7 +502,6 @@
             pltpu.SemaphoreType.DMA,
             pltpu.SemaphoreType.DMA,
             pltpu.SemaphoreType.REGULAR,
-            pltpu.SemaphoreType.REGULAR,
         ],
         compiler_params=pltpu.CompilerParams(
             collective_id=0, has_side_effects=True, vmem_limit_bytes=60 * 2**20

time: 46.9 us -> 40.5 us (0.86)
  the two profiles are of different devices: /device:TPU:17 before, /device:TPU:8 now
where the time goes in v5:
time: 40.5 us; the launch traced here: 40.3 us
  Pallas kernels  37.3 us (92%)
  local copies, waits for them, and re-layouts  1.71 us (4%)
  between operations  1.31 us (3%)
    pallas_call x1, Pallas kernels  37.3 us
    unnamed x6, local copies, waits for them, and re-layouts  1.71 us

profile of v5, /device:TPU:8, one launch (start us, length us, event | category | flops | bytes accessed | tf_op | source)
XLA Modules:
  0.0 40.3 jit_solution(17399221989772025719)
XLA Ops:
  1.3 37.3 %shard_map.122 = (f32[64]{0:T(128)}, f32[3,64]{1,0:T(4,128)}) custom-call(f32[3,64]{1,0:T(4,128)} %pos_hbm.1, s32[64]{0:T(128)} %spc_hbm.1, bf16[64,128]{1,0:T(8,128)(2,1)} %node_hbm.1, bf16[128,128]{1,0:T(8,128)(2,1)} %wself_hbm.1, bf16[128,128]{1,0:T(8,128)(2,1)} %wsend_hbm.1, f32[8,128]{1,0:T(8,128)} %radial_hbm.1, bf16[128,128]{1,0:T(8,128)(2,1)} %wmix_hbm.1, ...), custom_call_target="tpu_custom_call" | custom-call | tf_op jit(solution)/shard_map/pallas_call
  38.6 0.0 copy-start.1
  38.6 0.0 copy-start
  38.6 0.6 %copy-done.1 = f32[64]{0:T(128)S(1)} copy-done((f32[64]{0:T(128)S(1)}, f32[64]{0:T(128)}, u32[]{:S(2)}) %copy-start.1) | copy-done | bytes 280
  39.2 0.5 %copy.16 = f32[64]{0:T(128)} copy(f32[64]{0:T(128)S(1)} %copy-done.1) | data formatting | bytes 512
  39.7 0.0 copy-done
  39.7 0.6 %copy.17 = f32[3,64]{1,0:T(4,128)} copy(f32[3,64]{1,0:T(4,128)S(1)} %copy-done) | data formatting | bytes 1536
Async XLA Ops:
  38.6 0.6 %copy-start.1 = (f32[64]{0:T(128)S(1)}, f32[64]{0:T(128)}, u32[]{:S(2)}) copy-start(f32[64]{0:T(128)} %get-tuple-element.4) | copy-start | bytes 772
  38.6 1.1 %copy-start = (f32[3,64]{1,0:T(4,128)S(1)}, f32[3,64]{1,0:T(4,128)}, u32[]{:S(2)}) copy-start(f32[3,64]{1,0:T(4,128)} %get-tuple-element.5) | copy-start | bytes 2308

commit v6 on v5

--- a/solution.py
+++ b/solution.py
@@ -14,6 +14,8 @@
 CHUNK = 1024
 CENTRES = CHUNK // BLOCK
 SPACING = 2.5 / 7
+ROWS_OF_PAIRS = PAIRS // 128
+ROOT = 1.4426950408889634**0.5
 MESH = pl.DeviceIdType.MESH
 BF16, F32 = jnp.bfloat16, jnp.float32
 
@@ -68,10 +70,10 @@
     near,
     asked,
     centres,
-    block_ref,
-    pos_exp,
-    scale_exp,
-    hot_centre,
+    spread,
+    scaled_ref,
+    slope_ref,
+    energy_rows,
     rhs_pair,
     rhs_centre,
     lhs_send,
@@ -134,11 +136,6 @@
     for load in loads:
         load.start()
 
-    def spread_hot(step, carry):
-        lanes = pl.ds(pl.multiple_of(step * CHUNK, CHUNK), CHUNK)
-        hot_centre[:, lanes] = centre_onehot(step * CHUNK, CHUNK).astype(BF16)
-        return carry
-
     for load in loads[:7]:
         load.wait()
 
@@ -170,6 +167,7 @@
     asked[1, BLOCK:ROWS, :] = place
     asked[1, ROWS : ROWS + 3 * members, :] = slots_in(1, 1 - core)
     asked[1, ROWS + 3 * members :, :] = slots_in(2 - 2 * core, 1 - core)
+    asked[0, ROWS + 3 * members :, :] = jnp.zeros((3 * members, C), F32)
 
     @pl.when(core == 1)
     def _():
@@ -215,7 +213,6 @@
 
     pl.when(jnp.logical_not(early))(ask_far)
 
-    lax.fori_loop(0, PAIRS // CHUNK, spread_hot, 0)
     atom = lax.broadcasted_iota(jnp.int32, (BLOCK, CHUNK), 0)
     lane = lax.broadcasted_iota(jnp.int32, (BLOCK, CHUNK), 1)
     hot_j = jnp.where(lax.rem(lane, BLOCK) == atom, 1.0, 0.0).astype(F32)
@@ -241,15 +238,22 @@
     near_grads[...] = jnp.zeros_like(near_grads)
 
     row8 = lax.broadcasted_iota(jnp.int32, (8, BLOCK), 0)
-    row = lax.broadcasted_iota(jnp.int32, (8, CHUNK), 0)
-    pair = lax.broadcasted_iota(jnp.int32, (1, CHUNK), 1)
-    center = row.astype(F32) * SPACING
-    gap = lax.rem(pair, BLOCK) - pair // BLOCK
+    center = lax.broadcasted_iota(jnp.int32, (8, CHUNK), 0).astype(F32) * ROOT
+    line = lax.broadcasted_iota(jnp.int32, (ROWS_OF_PAIRS, BLOCK), 0)
+    atom = lax.broadcasted_iota(jnp.int32, (ROWS_OF_PAIRS, BLOCK), 1)
+    on_line = jnp.where(atom // 2 == line, 1.0, 0.0)
+    lane = lax.broadcasted_iota(jnp.int32, (BLOCK, C), 1)
+    atom = lax.broadcasted_iota(jnp.int32, (BLOCK, C), 0)
+    in_half = jnp.where(lax.rem(atom, 2) == lane // BLOCK, 1.0, 0.0).astype(BF16)
+    line = lax.broadcasted_iota(jnp.int32, (ROWS_OF_PAIRS, C), 0)
+    lane = lax.broadcasted_iota(jnp.int32, (ROWS_OF_PAIRS, C), 1)
+    same_atom = jnp.where(2 * line + lane // BLOCK == lax.rem(lane, BLOCK), 1.0, 0.0)
     mates_blocks = own.at[pl.ds(0, members - 1)]
     mates_grads = grads.at[pl.ds(0, members - 1)]
 
     pltpu.make_async_copy(mates_blocks, mates_blocks, own_recv_sem).wait()
     lend.start()
+    lend.wait_recv()
 
     def group(turn, carry):
         which = jnp.where(early, 1 - turn, turn)
@@ -257,10 +261,6 @@
         @pl.when(which == 0)
         def _():
             ask.wait_recv()
-
-        @pl.when(which == 1)
-        def _():
-            lend.wait_recv()
 
         spot = asked[which, BLOCK:ROWS, 0:BLOCK]
         scale8 = jnp.zeros((8, BLOCK), F32)
@@ -268,71 +268,68 @@
             for s in range(4):
                 there = (row8 == s) & (spot[3:4] == float(r))
                 scale8 = jnp.where(there, scale_ref[r, s], scale8)
-        small = jnp.concatenate(parts(spot, 3) + parts(scale8, 3), axis=0).astype(BF16)
+        wide = []
+        for values in [spot[k : k + 1] for k in range(3)] + [scale8[k : k + 1] for k in range(4)]:
+            wide += [on_line * part for part in parts(values, 3)]
+        found = dot(jnp.concatenate(wide, axis=0).astype(BF16), in_half)
+        for k in range(7):
+            base = k * 3 * ROWS_OF_PAIRS
+            one, two, three = (
+                found[base + p * ROWS_OF_PAIRS : base + (p + 1) * ROWS_OF_PAIRS] for p in range(3)
+            )
+            spread[k] = one + two + three
         half_hi, half_lo = parts(radial_ref[...] * 0.5, 2)
         for k in range(PAIRS // CHUNK):
             mine = pl.ds(k * CENTRES, CENTRES)
             self_hi, self_lo = parts(asked[which, mine, :] * 0.5, 2)
             rest = [half_hi, half_lo, half_hi, jnp.zeros((8, C), F32), self_hi, self_lo]
             lhs_rest[k] = jnp.concatenate(rest, axis=0).T.astype(BF16)
-            lanes = slice(k * CHUNK, (k + 1) * CHUNK)
-            spread = dot(small, hot_centre[:, lanes])
-            pos_exp[:, lanes] = spread[0:8] + spread[8:16] + spread[16:24]
-            scale_exp[:, lanes] = spread[24:32] + spread[32:40] + spread[40:48]
         pair_acc[...] = jnp.zeros_like(pair_acc)
 
         def tile(slot, carry):
-            @pl.when(early & (which == 1) & (slot == 1))
+            @pl.when(early & (which == 1) & (slot == 0))
             def _():
                 ask_far()
 
             hot_rows = pl.ds(pl.multiple_of(ROWS + slot * members, 8), members)
             near_rows = pl.ds(pl.multiple_of(ROWS + (slot + 3) * members, 8), members)
             hot = asked[which, hot_rows, :]
-            live = jnp.sum(hot, axis=0, keepdims=True)
+            near_hot = asked[which, near_rows, :]
+            live = jnp.sum(hot + near_hot, axis=0, keepdims=True)
             self_hot = asked[which, pl.ds(ROWS + slot * members + me, 1), :]
             self_hot = jnp.where(which == 1, self_hot, 0.0)
-            self_hot = jnp.concatenate([self_hot] * (CHUNK // C), axis=1)
-            chosen = own[0] * hot[0:1]
+            block = own[0] * hot[0:1] + near[0] * near_hot[0:1]
             for k in range(1, members):
-                chosen = chosen + own[k] * hot[k : k + 1]
-            block_ref[0:ROWS, :] = chosen
-            block_ref[ROWS:, :] = jnp.broadcast_to(live, (8, C))
-
-            @pl.when(which == 1)
-            def _():
-                near_hot = asked[which, near_rows, :]
-                chosen = block_ref[0:ROWS, :]
-                for k in range(members):
-                    chosen = chosen + near[k] * near_hot[k : k + 1]
-                block_ref[0:ROWS, :] = chosen
-                near_live = jnp.sum(near_hot, axis=0, keepdims=True)
-                block_ref[ROWS:, :] += jnp.broadcast_to(near_live, (8, C))
-
-            block = block_ref[0:ROWS, :]
-            live = jnp.concatenate([block_ref[ROWS : ROWS + 1, :]] * (CHUNK // C), axis=1)
-            place_j = jnp.concatenate([block[BLOCK:ROWS, 0:BLOCK]] * (CHUNK // BLOCK), axis=1)
-            kind_hot = jnp.where(place_j[3:4] == row.astype(F32), 1.0, 0.0)
+                block = block + own[k] * hot[k : k + 1] + near[k] * near_hot[k : k + 1]
             lhs_send[...] = jnp.concatenate(parts(block[0:BLOCK] * 0.5, 2), axis=0).T.astype(BF16)
+            place_j = block[BLOCK:ROWS, 0:BLOCK]
+            place_j = jnp.concatenate([place_j, place_j], axis=1)
+            diff = [place_j[k : k + 1] - spread[k] for k in range(3)]
+            dist_sq = diff[0] * diff[0] + diff[1] * diff[1] + diff[2] * diff[2]
+            kind = place_j[3:4]
+            scale = jnp.where(
+                kind == 0.0,
+                spread[3],
+                jnp.where(kind == 1.0, spread[4], jnp.where(kind == 2.0, spread[5], spread[6])),
+            )
+            scaled = dist_sq * scale
+            scaled_ref[...] = scaled * (ROOT / SPACING)
+            keep = live - self_hot * same_atom
+            reach = jnp.maximum(1.0 - scaled * (1.0 / 2.5), 0.0)
 
             def first(turn):
-                lanes = slice(turn * CHUNK, (turn + 1) * CHUNK)
-                diff = jnp.where(row < 3, place_j - pos_exp[:, lanes], 0.0)
-                dist_sq = jnp.sum(diff * diff, axis=0, keepdims=True)
-                scale = jnp.sum(scale_exp[:, lanes] * kind_hot, axis=0, keepdims=True)
-                scaled = dist_sq * scale
-                keep = live - jnp.where(gap == turn * CENTRES, self_hot, 0.0)
-                reach = jnp.maximum(1.0 - scaled * (1.0 / 2.5), 0.0)
-                offset = (scaled - center) * (1.0 / SPACING)
-                basis = jnp.exp(-(offset * offset))
-                slope = basis * offset * (-2.0 / SPACING)
+                base = turn * (CHUNK // C)
+                wide = [scaled_ref[base + k : base + k + 1, :] for k in range(CHUNK // C)]
+                offset = jnp.concatenate(wide, axis=1) - center
+                basis = jnp.exp2(-(offset * offset))
+                slope = basis * offset
                 basis_hi, basis_lo = parts(basis, 2)
                 head = jnp.concatenate(
                     [basis_hi, basis_hi, basis_lo, jnp.zeros((8, CHUNK), F32)], axis=0
                 ).astype(BF16)
                 rhs = jnp.concatenate([rhs_pair[...], head, rhs_centre[...]], axis=0)
                 lhs = jnp.concatenate([lhs_send[...], lhs_rest[turn]], axis=1)
-                return lanes, diff, scale, keep, reach, slope, dot(lhs, rhs)
+                return base, slope, dot(lhs, rhs)
 
             def second(state):
                 half = state[-1]
@@ -348,38 +345,38 @@
                 t = jnp.tanh(half)
                 p = (1.0 + t) * jnp.concatenate([ro_exp[...]] * (CHUNK // C), axis=1)
                 mixed = half * p
-                slope_2 = p + mixed * (1.0 - t)
-                out = dot(lhs_b[...], jnp.concatenate([mixed, slope_2], axis=0).astype(BF16))
+                mixed = mixed.astype(BF16)
+                slope_2 = p.astype(BF16) + mixed * (1.0 - t.astype(BF16))
+                out = dot(lhs_b[...], jnp.concatenate([mixed, slope_2], axis=0))
                 return state[:-1] + (out,)
 
             def fourth(state):
-                lanes, diff, scale, keep, reach, slope, slope_1, out = state
+                base, slope, slope_1, out = state
                 d_basis = dot(lhs_r[...], (out[0:C] * slope_1).astype(BF16))
-                d_basis = d_basis[0:8] + d_basis[8:16]
-                energy = out[C : C + 1]
-                cut = reach * reach
-                d_scaled = cut * jnp.sum(d_basis * slope, axis=0, keepdims=True)
-                d_scaled = d_scaled - (2.0 / 2.5) * reach * energy
-                force = (2.0 * keep * scale * d_scaled) * diff
-                found = jnp.where(row == 3, keep * cut * energy, force)
-                pair_acc[:, lanes] += found
-                total = found[:, 0:C]
-                for k in range(1, CHUNK // C):
-                    total = total + found[:, k * C : (k + 1) * C]
-                return total
+                slope = jnp.sum((d_basis[0:8] + d_basis[8:16]) * slope, axis=0, keepdims=True)
+                for k in range(CHUNK // C):
+                    lanes = slice(k * C, (k + 1) * C)
+                    slope_ref[base + k : base + k + 1, :] = slope[:, lanes]
+                    energy_rows[base + k : base + k + 1, :] = out[C : C + 1, lanes]
 
             stages = [first, second, third, fourth]
             states = {}
-            total = None
             count = PAIRS // CHUNK
             for turn in range(count + 3):
                 for depth in range(4):
                     sub = turn - depth
                     if 0 <= sub < count:
                         states[sub] = stages[depth](states.get(sub, sub))
-                        if depth == 3:
-                            part = states.pop(sub)
-                            total = part if total is None else total + part
+            energy = energy_rows[...]
+            cut = reach * reach
+            d_scaled = cut * slope_ref[...] * (-2.0 / (SPACING * ROOT))
+            d_scaled = 2.0 * keep * scale * (d_scaled - (2.0 / 2.5) * reach * energy)
+            found = [d_scaled * part for part in diff]
+            for k in range(3):
+                pair_acc[k] += found[k]
+            pair_acc[3] += keep * cut * energy
+            total = [jnp.sum(part, axis=0, keepdims=True) for part in found]
+            total = jnp.concatenate(total + [jnp.zeros((5, C), F32)], axis=0)
             grad = total[:, 0:BLOCK] + total[:, BLOCK:C]
             grad = jnp.concatenate([grad, jnp.zeros_like(grad)], axis=1)
             for k in range(members):
@@ -387,7 +384,6 @@
 
             @pl.when(which == 1)
             def _():
-                near_hot = asked[which, near_rows, :]
                 for k in range(members):
                     near_grads[k] += grad * near_hot[k : k + 1]
 
@@ -395,17 +391,23 @@
 
         lax.fori_loop(0, 3, tile, 0)
 
-        total = jnp.zeros((24, BLOCK), F32)
-        for k in range(PAIRS // CHUNK):
-            lanes = slice(k * CHUNK, (k + 1) * CHUNK)
-            split = jnp.concatenate(parts(pair_acc[:, lanes], 3), axis=0).astype(BF16)
-            total = total + lax.dot_general(
-                split,
-                hot_centre[:, lanes],
-                (((1,), (1,)), ((), ())),
-                preferred_element_type=F32,
+        wide = []
+        for k in range(4):
+            wide += parts(pair_acc[k], 3)
+        found = lax.dot_general(
+            jnp.concatenate(wide, axis=0).astype(BF16),
+            in_half,
+            (((1,), (1,)), ((), ())),
+            preferred_element_type=F32,
+        )
+        total = []
+        for k in range(4):
+            base = k * 3 * ROWS_OF_PAIRS
+            one, two, three = (
+                found[base + p * ROWS_OF_PAIRS : base + (p + 1) * ROWS_OF_PAIRS] for p in range(3)
             )
-        total = total[0:8] + total[8:16] + total[16:24]
+            total.append(jnp.sum((one + two + three) * on_line, axis=0, keepdims=True))
+        total = jnp.concatenate(total + [jnp.zeros((4, BLOCK), F32)], axis=0)
         centre_sums[which] = jnp.concatenate([total, jnp.zeros_like(total)], axis=1)
 
         @pl.when(which == 0)
@@ -475,10 +477,10 @@
             pltpu.VMEM((members, ROWS, C), F32),
             pltpu.VMEM((2, ROWS + 6 * members, C), F32),
             pltpu.VMEM((ROWS + 3 * members, C), F32),
-            pltpu.VMEM((ROWS + 8, C), F32),
-            pltpu.VMEM((8, PAIRS), F32),
-            pltpu.VMEM((8, PAIRS), F32),
-            pltpu.VMEM((BLOCK, PAIRS), BF16),
+            pltpu.VMEM((7, ROWS_OF_PAIRS, C), F32),
+            pltpu.VMEM((ROWS_OF_PAIRS, C), F32),
+            pltpu.VMEM((ROWS_OF_PAIRS, C), F32),
+            pltpu.VMEM((ROWS_OF_PAIRS, C), F32),
             pltpu.VMEM((2 * BLOCK, CHUNK), BF16),
             pltpu.VMEM((2 * CENTRES, CHUNK), BF16),
             pltpu.VMEM((C, 2 * BLOCK), BF16),
@@ -487,7 +489,7 @@
             pltpu.VMEM((16, C), BF16),
             pltpu.VMEM((C, C), BF16),
             pltpu.VMEM((C, C), F32),
-            pltpu.VMEM((8, PAIRS), F32),
+            pltpu.VMEM((4, ROWS_OF_PAIRS, C), F32),
             pltpu.VMEM((2, 8, C), F32),
             pltpu.VMEM((members, 8, C), F32),
             pltpu.VMEM((members, 8, C), F32),

time: 40.5 us -> 40.6 us (level)
  the two profiles are of different devices: /device:TPU:8 before, /device:TPU:1 now
where the time goes in v6:
time: 40.6 us; the launch traced here: 40.3 us
  Pallas kernels  37.3 us (92%)
  local copies, waits for them, and re-layouts  1.71 us (4%)
  between operations  1.31 us (3%)
    pallas_call x1, Pallas kernels  37.3 us
    unnamed x6, local copies, waits for them, and re-layouts  1.71 us

profile of v6, /device:TPU:1, one launch (start us, length us, event | category | flops | bytes accessed | tf_op | source)
XLA Modules:
  0.0 40.3 jit_solution(7830742252809448202)
XLA Ops:
  1.3 37.3 %shard_map.122 = (f32[64]{0:T(128)}, f32[3,64]{1,0:T(4,128)}) custom-call(f32[3,64]{1,0:T(4,128)} %pos_hbm.1, s32[64]{0:T(128)} %spc_hbm.1, bf16[64,128]{1,0:T(8,128)(2,1)} %node_hbm.1, bf16[128,128]{1,0:T(8,128)(2,1)} %wself_hbm.1, bf16[128,128]{1,0:T(8,128)(2,1)} %wsend_hbm.1, f32[8,128]{1,0:T(8,128)} %radial_hbm.1, bf16[128,128]{1,0:T(8,128)(2,1)} %wmix_hbm.1, ...), custom_call_target="tpu_custom_call" | custom-call | tf_op jit(solution)/shard_map/pallas_call
  38.6 0.0 copy-start.1
  38.6 0.0 copy-start
  38.6 0.6 %copy-done.1 = f32[64]{0:T(128)S(1)} copy-done((f32[64]{0:T(128)S(1)}, f32[64]{0:T(128)}, u32[]{:S(2)}) %copy-start.1) | copy-done | bytes 280
  39.2 0.5 %copy.16 = f32[64]{0:T(128)} copy(f32[64]{0:T(128)S(1)} %copy-done.1) | data formatting | bytes 512
  39.8 0.0 copy-done
  39.8 0.6 %copy.17 = f32[3,64]{1,0:T(4,128)} copy(f32[3,64]{1,0:T(4,128)S(1)} %copy-done) | data formatting | bytes 1536
Async XLA Ops:
  38.6 0.6 %copy-start.1 = (f32[64]{0:T(128)S(1)}, f32[64]{0:T(128)}, u32[]{:S(2)}) copy-start(f32[64]{0:T(128)} %get-tuple-element.4) | copy-start | bytes 772
  38.6 1.1 %copy-start = (f32[3,64]{1,0:T(4,128)S(1)}, f32[3,64]{1,0:T(4,128)}, u32[]{:S(2)}) copy-start(f32[3,64]{1,0:T(4,128)} %get-tuple-element.5) | copy-start | bytes 2308

commit v7 on v6

--- a/solution.py
+++ b/solution.py
@@ -11,7 +11,7 @@
 C = 128
 ROWS = 72
 PAIRS = BLOCK * BLOCK
-CHUNK = 1024
+CHUNK = 512
 CENTRES = CHUNK // BLOCK
 SPACING = 2.5 / 7
 ROWS_OF_PAIRS = PAIRS // 128
@@ -85,6 +85,7 @@
     pair_acc,
     centre_sums,
     grads,
+    near_sum,
     near_grads,
     near_back,
     returned,
@@ -235,7 +236,7 @@
     readout = readout_ref[...].reshape(1, C)
     ro_exp[...] = jnp.broadcast_to(readout, (C, C)).T
     grads[...] = jnp.zeros_like(grads)
-    near_grads[...] = jnp.zeros_like(near_grads)
+    near_sum[...] = jnp.zeros_like(near_sum)
 
     row8 = lax.broadcasted_iota(jnp.int32, (8, BLOCK), 0)
     center = lax.broadcasted_iota(jnp.int32, (8, CHUNK), 0).astype(F32) * ROOT
@@ -286,13 +287,13 @@
             lhs_rest[k] = jnp.concatenate(rest, axis=0).T.astype(BF16)
         pair_acc[...] = jnp.zeros_like(pair_acc)
 
-        def tile(slot, carry):
-            @pl.when(early & (which == 1) & (slot == 0))
-            def _():
-                ask_far()
-
-            hot_rows = pl.ds(pl.multiple_of(ROWS + slot * members, 8), members)
-            near_rows = pl.ds(pl.multiple_of(ROWS + (slot + 3) * members, 8), members)
+        @pl.when(early & (which == 1))
+        def _():
+            ask_far()
+
+        def begin(slot):
+            hot_rows = pl.ds(ROWS + slot * members, members)
+            near_rows = pl.ds(ROWS + (slot + 3) * members, members)
             hot = asked[which, hot_rows, :]
             near_hot = asked[which, near_rows, :]
             live = jnp.sum(hot + near_hot, axis=0, keepdims=True)
@@ -301,7 +302,7 @@
             block = own[0] * hot[0:1] + near[0] * near_hot[0:1]
             for k in range(1, members):
                 block = block + own[k] * hot[k : k + 1] + near[k] * near_hot[k : k + 1]
-            lhs_send[...] = jnp.concatenate(parts(block[0:BLOCK] * 0.5, 2), axis=0).T.astype(BF16)
+            lhs_send[slot] = jnp.concatenate(parts(block[0:BLOCK] * 0.5, 2), axis=0).T.astype(BF16)
             place_j = block[BLOCK:ROWS, 0:BLOCK]
             place_j = jnp.concatenate([place_j, place_j], axis=1)
             diff = [place_j[k : k + 1] - spread[k] for k in range(3)]
@@ -313,63 +314,58 @@
                 jnp.where(kind == 1.0, spread[4], jnp.where(kind == 2.0, spread[5], spread[6])),
             )
             scaled = dist_sq * scale
-            scaled_ref[...] = scaled * (ROOT / SPACING)
+            scaled_ref[slot] = scaled * (ROOT / SPACING)
             keep = live - self_hot * same_atom
             reach = jnp.maximum(1.0 - scaled * (1.0 / 2.5), 0.0)
-
-            def first(turn):
-                base = turn * (CHUNK // C)
-                wide = [scaled_ref[base + k : base + k + 1, :] for k in range(CHUNK // C)]
-                offset = jnp.concatenate(wide, axis=1) - center
-                basis = jnp.exp2(-(offset * offset))
-                slope = basis * offset
-                basis_hi, basis_lo = parts(basis, 2)
-                head = jnp.concatenate(
-                    [basis_hi, basis_hi, basis_lo, jnp.zeros((8, CHUNK), F32)], axis=0
-                ).astype(BF16)
-                rhs = jnp.concatenate([rhs_pair[...], head, rhs_centre[...]], axis=0)
-                lhs = jnp.concatenate([lhs_send[...], lhs_rest[turn]], axis=1)
-                return base, slope, dot(lhs, rhs)
-
-            def second(state):
-                half = state[-1]
-                t = jnp.tanh(half)
-                p = 1.0 + t
-                hidden = half * p
-                slope_1 = p + hidden * (1.0 - t)
-                half = dot(lhs_m[...], hidden.astype(BF16))
-                return state[:-1] + (slope_1, half)
-
-            def third(state):
-                half = state[-1]
-                t = jnp.tanh(half)
-                p = (1.0 + t) * jnp.concatenate([ro_exp[...]] * (CHUNK // C), axis=1)
-                mixed = half * p
-                mixed = mixed.astype(BF16)
-                slope_2 = p.astype(BF16) + mixed * (1.0 - t.astype(BF16))
-                out = dot(lhs_b[...], jnp.concatenate([mixed, slope_2], axis=0))
-                return state[:-1] + (out,)
-
-            def fourth(state):
-                base, slope, slope_1, out = state
-                d_basis = dot(lhs_r[...], (out[0:C] * slope_1).astype(BF16))
-                slope = jnp.sum((d_basis[0:8] + d_basis[8:16]) * slope, axis=0, keepdims=True)
-                for k in range(CHUNK // C):
-                    lanes = slice(k * C, (k + 1) * C)
-                    slope_ref[base + k : base + k + 1, :] = slope[:, lanes]
-                    energy_rows[base + k : base + k + 1, :] = out[C : C + 1, lanes]
-
-            stages = [first, second, third, fourth]
-            states = {}
-            count = PAIRS // CHUNK
-            for turn in range(count + 3):
-                for depth in range(4):
-                    sub = turn - depth
-                    if 0 <= sub < count:
-                        states[sub] = stages[depth](states.get(sub, sub))
-            energy = energy_rows[...]
+            return hot, near_hot, diff, scale, keep, reach
+
+        def first(slot, turn):
+            base = turn * (CHUNK // C)
+            wide = [scaled_ref[slot, base + k : base + k + 1, :] for k in range(CHUNK // C)]
+            offset = jnp.concatenate(wide, axis=1) - center
+            basis = jnp.exp2(-(offset * offset))
+            slope = basis * offset
+            basis_hi, basis_lo = parts(basis, 2)
+            head = jnp.concatenate(
+                [basis_hi, basis_hi, basis_lo, jnp.zeros((8, CHUNK), F32)], axis=0
+            ).astype(BF16)
+            rhs = jnp.concatenate([rhs_pair[...], head, rhs_centre[...]], axis=0)
+            lhs = jnp.concatenate([lhs_send[slot], lhs_rest[turn]], axis=1)
+            return slot, base, slope, dot(lhs, rhs)
+
+        def second(state):
+            half = state[-1]
+            t = jnp.tanh(half)
+            p = 1.0 + t
+            hidden = half * p
+            slope_1 = p + hidden * (1.0 - t)
+            half = dot(lhs_m[...], hidden.astype(BF16))
+            return state[:-1] + (slope_1, half)
+
+        def third(state):
+            half = state[-1]
+            t = jnp.tanh(half)
+            p = (1.0 + t) * jnp.concatenate([ro_exp[...]] * (CHUNK // C), axis=1)
+            mixed = half * p
+            mixed = mixed.astype(BF16)
+            slope_2 = p.astype(BF16) + mixed * (1.0 - t.astype(BF16))
+            out = dot(lhs_b[...], jnp.concatenate([mixed, slope_2], axis=0))
+            return state[:-1] + (out,)
+
+        def fourth(state):
+            slot, base, slope, slope_1, out = state
+            d_basis = dot(lhs_r[...], (out[0:C] * slope_1).astype(BF16))
+            slope = jnp.sum((d_basis[0:8] + d_basis[8:16]) * slope, axis=0, keepdims=True)
+            for k in range(CHUNK // C):
+                lanes = slice(k * C, (k + 1) * C)
+                slope_ref[slot, base + k : base + k + 1, :] = slope[:, lanes]
+                energy_rows[slot, base + k : base + k + 1, :] = out[C : C + 1, lanes]
+
+        def finish(slot, known):
+            hot, near_hot, diff, scale, keep, reach = known
+            energy = energy_rows[slot]
             cut = reach * reach
-            d_scaled = cut * slope_ref[...] * (-2.0 / (SPACING * ROOT))
+            d_scaled = cut * slope_ref[slot] * (-2.0 / (SPACING * ROOT))
             d_scaled = 2.0 * keep * scale * (d_scaled - (2.0 / 2.5) * reach * energy)
             found = [d_scaled * part for part in diff]
             for k in range(3):
@@ -381,15 +377,27 @@
             grad = jnp.concatenate([grad, jnp.zeros_like(grad)], axis=1)
             for k in range(members):
                 grads[k] += grad * hot[k : k + 1]
-
-            @pl.when(which == 1)
-            def _():
-                for k in range(members):
-                    near_grads[k] += grad * near_hot[k : k + 1]
-
-            return carry
-
-        lax.fori_loop(0, 3, tile, 0)
+                near_sum[k] += grad * near_hot[k : k + 1]
+
+        stages = [first, second, third, fourth]
+        count = PAIRS // CHUNK
+        known, states = {}, {}
+        for turn in range(3 * count + 3):
+            for depth in range(4):
+                sub = turn - depth
+                if not 0 <= sub < 3 * count:
+                    continue
+                slot, part = divmod(sub, count)
+                if depth == 0:
+                    if sub == 0:
+                        known[0] = begin(0)
+                    if part == count - 1 and slot < 2:
+                        known[slot + 1] = begin(slot + 1)
+                    states[sub] = first(slot, part)
+                else:
+                    states[sub] = stages[depth](states[sub])
+                if depth == 3 and part == count - 1:
+                    finish(slot, known.pop(slot))
 
         wide = []
         for k in range(4):
@@ -416,6 +424,7 @@
 
         @pl.when(which == 1)
         def _():
+            near_grads[...] = near_sum[...]
             repay.start()
 
         return carry
@@ -478,12 +487,12 @@
             pltpu.VMEM((2, ROWS + 6 * members, C), F32),
             pltpu.VMEM((ROWS + 3 * members, C), F32),
             pltpu.VMEM((7, ROWS_OF_PAIRS, C), F32),
-            pltpu.VMEM((ROWS_OF_PAIRS, C), F32),
-            pltpu.VMEM((ROWS_OF_PAIRS, C), F32),
-            pltpu.VMEM((ROWS_OF_PAIRS, C), F32),
+            pltpu.VMEM((3, ROWS_OF_PAIRS, C), F32),
+            pltpu.VMEM((3, ROWS_OF_PAIRS, C), F32),
+            pltpu.VMEM((3, ROWS_OF_PAIRS, C), F32),
             pltpu.VMEM((2 * BLOCK, CHUNK), BF16),
             pltpu.VMEM((2 * CENTRES, CHUNK), BF16),
-            pltpu.VMEM((C, 2 * BLOCK), BF16),
+            pltpu.VMEM((3, C, 2 * BLOCK), BF16),
             pltpu.VMEM((PAIRS // CHUNK, C, 32 + 2 * CENTRES), BF16),
             pltpu.VMEM((C + 16, 2 * C), BF16),
             pltpu.VMEM((16, C), BF16),
@@ -491,6 +500,7 @@
             pltpu.VMEM((C, C), F32),
             pltpu.VMEM((4, ROWS_OF_PAIRS, C), F32),
             pltpu.VMEM((2, 8, C), F32),
+            pltpu.VMEM((members, 8, C), F32),
             pltpu.VMEM((members, 8, C), F32),
             pltpu.VMEM((members, 8, C), F32),
             pltpu.VMEM((members, 8, C), F32),

time: 40.6 us -> 37.8 us (0.931)
  Pallas kernels: 37.3 us -> 34.6 us
    pallas_call x1, Pallas kernels: 37.3 us -> 34.6 us
where the time goes in v7:
time: 37.8 us; the launch traced here: 37.6 us
  Pallas kernels  34.6 us (92%)
  local copies, waits for them, and re-layouts  1.71 us (5%)
  between operations  1.31 us (3%)
    pallas_call x1, Pallas kernels  34.6 us
    unnamed x6, local copies, waits for them, and re-layouts  1.71 us

profile of v7, /device:TPU:1, one launch (start us, length us, event | category | flops | bytes accessed | tf_op | source)
XLA Modules:
  0.0 37.6 jit_solution(2498772794352552088)
XLA Ops:
  1.3 34.6 %shard_map.122 = (f32[64]{0:T(128)}, f32[3,64]{1,0:T(4,128)}) custom-call(f32[3,64]{1,0:T(4,128)} %pos_hbm.1, s32[64]{0:T(128)} %spc_hbm.1, bf16[64,128]{1,0:T(8,128)(2,1)} %node_hbm.1, bf16[128,128]{1,0:T(8,128)(2,1)} %wself_hbm.1, bf16[128,128]{1,0:T(8,128)(2,1)} %wsend_hbm.1, f32[8,128]{1,0:T(8,128)} %radial_hbm.1, bf16[128,128]{1,0:T(8,128)(2,1)} %wmix_hbm.1, ...), custom_call_target="tpu_custom_call" | custom-call | tf_op jit(solution)/shard_map/pallas_call
  35.9 0.0 copy-start.1
  35.9 0.0 copy-start
  35.9 0.6 %copy-done.1 = f32[64]{0:T(128)S(1)} copy-done((f32[64]{0:T(128)S(1)}, f32[64]{0:T(128)}, u32[]{:S(2)}) %copy-start.1) | copy-done | bytes 280
  36.5 0.5 %copy.16 = f32[64]{0:T(128)} copy(f32[64]{0:T(128)S(1)} %copy-done.1) | data formatting | bytes 512
  37.0 0.0 copy-done
  37.0 0.6 %copy.17 = f32[3,64]{1,0:T(4,128)} copy(f32[3,64]{1,0:T(4,128)S(1)} %copy-done) | data formatting | bytes 1536
Async XLA Ops:
  35.9 0.6 %copy-start.1 = (f32[64]{0:T(128)S(1)}, f32[64]{0:T(128)}, u32[]{:S(2)}) copy-start(f32[64]{0:T(128)} %get-tuple-element.4) | copy-start | bytes 772
  35.9 1.1 %copy-start = (f32[3,64]{1,0:T(4,128)S(1)}, f32[3,64]{1,0:T(4,128)}, u32[]{:S(2)}) copy-start(f32[3,64]{1,0:T(4,128)} %get-tuple-element.5) | copy-start | bytes 2308

commit v8 on v7

--- a/solution.py
+++ b/solution.py
@@ -68,6 +68,7 @@
     count_ref,
     own,
     near,
+    near_used,
     asked,
     centres,
     spread,
@@ -95,6 +96,8 @@
     recv_sem,
     own_send_sem,
     own_recv_sem,
+    near_send_sem,
+    near_recv_sem,
     back_send_sem,
     back_recv_sem,
     group_sem,
@@ -179,15 +182,29 @@
     def _():
         pl.semaphore_wait(group_sem, 1)
 
+    def arrival(member, to=me):
+        return pltpu.make_async_remote_copy(
+            src_ref=own.at[member],
+            dst_ref=own.at[member],
+            send_sem=own_send_sem,
+            recv_sem=own_recv_sem.at[member],
+            device_id=(slab, to),
+            device_id_type=MESH,
+        )
+
+    def lend(member):
+        return pltpu.make_async_remote_copy(
+            src_ref=own.at[member],
+            dst_ref=near.at[member],
+            send_sem=near_send_sem,
+            recv_sem=near_recv_sem.at[member],
+            device_id=(sib_slab, me),
+            device_id_type=MESH,
+        )
+
     for mate in mates:
-        pltpu.make_async_remote_copy(
-            src_ref=own.at[me],
-            dst_ref=own.at[me],
-            send_sem=own_send_sem,
-            recv_sem=own_recv_sem,
-            device_id=(slab, mate),
-            device_id_type=MESH,
-        ).start()
+        arrival(me, mate).start()
+    lend(me).start()
 
     def copy(index, source, target, to_slab):
         return pltpu.make_async_remote_copy(
@@ -201,8 +218,7 @@
 
     ask = copy(0, centres, asked.at[0, pl.ds(0, ROWS + 3 * members)], far_slab)
     tell = copy(1, centre_sums.at[0], returned, far_slab)
-    lend = copy(2, own, near, sib_slab)
-    repay = copy(3, near_grads, near_back, sib_slab)
+    repay = copy(2, near_grads, near_back, sib_slab)
     early = slab == 0
 
     def ask_far():
@@ -252,9 +268,10 @@
     mates_blocks = own.at[pl.ds(0, members - 1)]
     mates_grads = grads.at[pl.ds(0, members - 1)]
 
-    pltpu.make_async_copy(mates_blocks, mates_blocks, own_recv_sem).wait()
-    lend.start()
-    lend.wait_recv()
+    for mate in mates:
+        arrival(mate).wait_recv()
+        lend(mate).start()
+    pl.when(early)(ask_far)
 
     def group(turn, carry):
         which = jnp.where(early, 1 - turn, turn)
@@ -262,6 +279,13 @@
         @pl.when(which == 0)
         def _():
             ask.wait_recv()
+            near_used[...] = jnp.zeros_like(near_used)
+
+        @pl.when(which == 1)
+        def _():
+            for block in range(members):
+                lend(block).wait_recv()
+            near_used[...] = near[...]
 
         spot = asked[which, BLOCK:ROWS, 0:BLOCK]
         scale8 = jnp.zeros((8, BLOCK), F32)
@@ -287,10 +311,6 @@
             lhs_rest[k] = jnp.concatenate(rest, axis=0).T.astype(BF16)
         pair_acc[...] = jnp.zeros_like(pair_acc)
 
-        @pl.when(early & (which == 1))
-        def _():
-            ask_far()
-
         def begin(slot):
             hot_rows = pl.ds(ROWS + slot * members, members)
             near_rows = pl.ds(ROWS + (slot + 3) * members, members)
@@ -299,9 +319,9 @@
             live = jnp.sum(hot + near_hot, axis=0, keepdims=True)
             self_hot = asked[which, pl.ds(ROWS + slot * members + me, 1), :]
             self_hot = jnp.where(which == 1, self_hot, 0.0)
-            block = own[0] * hot[0:1] + near[0] * near_hot[0:1]
+            block = own[0] * hot[0:1] + near_used[0] * near_hot[0:1]
             for k in range(1, members):
-                block = block + own[k] * hot[k : k + 1] + near[k] * near_hot[k : k + 1]
+                block = block + own[k] * hot[k : k + 1] + near_used[k] * near_hot[k : k + 1]
             lhs_send[slot] = jnp.concatenate(parts(block[0:BLOCK] * 0.5, 2), axis=0).T.astype(BF16)
             place_j = block[BLOCK:ROWS, 0:BLOCK]
             place_j = jnp.concatenate([place_j, place_j], axis=1)
@@ -337,9 +357,10 @@
             half = state[-1]
             t = jnp.tanh(half)
             p = 1.0 + t
-            hidden = half * p
-            slope_1 = p + hidden * (1.0 - t)
-            half = dot(lhs_m[...], hidden.astype(BF16))
+            hidden = (half * p).astype(BF16)
+            t = t.astype(BF16)
+            slope_1 = (1.0 + t) + hidden * (1.0 - t)
+            half = dot(lhs_m[...], hidden)
             return state[:-1] + (slope_1, half)
 
         def third(state):
@@ -354,7 +375,7 @@
 
         def fourth(state):
             slot, base, slope, slope_1, out = state
-            d_basis = dot(lhs_r[...], (out[0:C] * slope_1).astype(BF16))
+            d_basis = dot(lhs_r[...], out[0:C].astype(BF16) * slope_1)
             slope = jnp.sum((d_basis[0:8] + d_basis[8:16]) * slope, axis=0, keepdims=True)
             for k in range(CHUNK // C):
                 lanes = slice(k * C, (k + 1) * C)
@@ -453,8 +474,9 @@
         total = total + back[k]
     force_ref[...] = (centre_sum - total)[0:3, 0:BLOCK]
 
-    for sent in (ask, tell, lend, repay):
+    for sent in (ask, tell, repay):
         sent.wait_send()
+    pltpu.make_async_copy(near, near, near_send_sem).wait()
     pltpu.make_async_copy(mates_blocks, mates_blocks, own_send_sem).wait()
     pltpu.make_async_copy(mates_grads, mates_grads, back_send_sem).wait()
 
@@ -484,6 +506,7 @@
             pltpu.SMEM((1,), jnp.int32),
             pltpu.VMEM((members, ROWS, C), F32),
             pltpu.VMEM((members, ROWS, C), F32),
+            pltpu.VMEM((members, ROWS, C), F32),
             pltpu.VMEM((2, ROWS + 6 * members, C), F32),
             pltpu.VMEM((ROWS + 3 * members, C), F32),
             pltpu.VMEM((7, ROWS_OF_PAIRS, C), F32),
@@ -507,10 +530,12 @@
             pltpu.VMEM((8, C), F32),
             pltpu.VMEM((members, 8, C), F32),
             pltpu.SemaphoreType.DMA((11,)),
-            pltpu.SemaphoreType.DMA((4,)),
-            pltpu.SemaphoreType.DMA((4,)),
+            pltpu.SemaphoreType.DMA((3,)),
+            pltpu.SemaphoreType.DMA((3,)),
             pltpu.SemaphoreType.DMA,
+            pltpu.SemaphoreType.DMA((members,)),
             pltpu.SemaphoreType.DMA,
+            pltpu.SemaphoreType.DMA((members,)),
             pltpu.SemaphoreType.DMA,
             pltpu.SemaphoreType.DMA,
             pltpu.SemaphoreType.REGULAR,

time: 37.8 us -> 35.8 us (0.947)
  the two profiles are of different devices: /device:TPU:1 before, /device:TPU:8 now
where the time goes in v8:
time: 35.8 us; the launch traced here: 35.6 us
  Pallas kernels  32.6 us (91%)
  local copies, waits for them, and re-layouts  1.71 us (5%)
  between operations  1.31 us (4%)
    pallas_call x1, Pallas kernels  32.6 us
    unnamed x6, local copies, waits for them, and re-layouts  1.71 us

profile of v8, /device:TPU:8, one launch (start us, length us, event | category | flops | bytes accessed | tf_op | source)
XLA Modules:
  0.0 35.6 jit_solution(15760850532123302678)
XLA Ops:
  1.3 32.6 %shard_map.122 = (f32[64]{0:T(128)}, f32[3,64]{1,0:T(4,128)}) custom-call(f32[3,64]{1,0:T(4,128)} %pos_hbm.1, s32[64]{0:T(128)} %spc_hbm.1, bf16[64,128]{1,0:T(8,128)(2,1)} %node_hbm.1, bf16[128,128]{1,0:T(8,128)(2,1)} %wself_hbm.1, bf16[128,128]{1,0:T(8,128)(2,1)} %wsend_hbm.1, f32[8,128]{1,0:T(8,128)} %radial_hbm.1, bf16[128,128]{1,0:T(8,128)(2,1)} %wmix_hbm.1, ...), custom_call_target="tpu_custom_call" | custom-call | tf_op jit(solution)/shard_map/pallas_call
  33.9 0.0 copy-start.1
  33.9 0.0 copy-start
  33.9 0.6 %copy-done.1 = f32[64]{0:T(128)S(1)} copy-done((f32[64]{0:T(128)S(1)}, f32[64]{0:T(128)}, u32[]{:S(2)}) %copy-start.1) | copy-done | bytes 280
  34.5 0.5 %copy.16 = f32[64]{0:T(128)} copy(f32[64]{0:T(128)S(1)} %copy-done.1) | data formatting | bytes 512
  35.0 0.0 copy-done
  35.0 0.6 %copy.17 = f32[3,64]{1,0:T(4,128)} copy(f32[3,64]{1,0:T(4,128)S(1)} %copy-done) | data formatting | bytes 1536
Async XLA Ops:
  33.9 0.6 %copy-start.1 = (f32[64]{0:T(128)S(1)}, f32[64]{0:T(128)}, u32[]{:S(2)}) copy-start(f32[64]{0:T(128)} %get-tuple-element.4) | copy-start | bytes 772
  33.9 1.1 %copy-start = (f32[3,64]{1,0:T(4,128)S(1)}, f32[3,64]{1,0:T(4,128)}, u32[]{:S(2)}) copy-start(f32[3,64]{1,0:T(4,128)} %get-tuple-element.5) | copy-start | bytes 2308

commit v9 on v8

--- a/solution.py
+++ b/solution.py
@@ -357,10 +357,9 @@
             half = state[-1]
             t = jnp.tanh(half)
             p = 1.0 + t
-            hidden = (half * p).astype(BF16)
-            t = t.astype(BF16)
-            slope_1 = (1.0 + t) + hidden * (1.0 - t)
-            half = dot(lhs_m[...], hidden)
+            hidden = half * p
+            slope_1 = p + hidden * (1.0 - t)
+            half = dot(lhs_m[...], hidden.astype(BF16))
             return state[:-1] + (slope_1, half)
 
         def third(state):
@@ -375,7 +374,7 @@
 
         def fourth(state):
             slot, base, slope, slope_1, out = state
-            d_basis = dot(lhs_r[...], out[0:C].astype(BF16) * slope_1)
+            d_basis = dot(lhs_r[...], (out[0:C] * slope_1).astype(BF16))
             slope = jnp.sum((d_basis[0:8] + d_basis[8:16]) * slope, axis=0, keepdims=True)
             for k in range(CHUNK // C):
                 lanes = slice(k * C, (k + 1) * C)

time: 35.8 us -> 36 us (level)
  no operation moved by 1% of the time
where the time goes in v9:
time: 36 us; the launch traced here: 35.8 us
  Pallas kernels  32.8 us (91%)
  local copies, waits for them, and re-layouts  1.71 us (5%)
  between operations  1.31 us (4%)
    pallas_call x1, Pallas kernels  32.8 us
    unnamed x6, local copies, waits for them, and re-layouts  1.71 us

profile of v9, /device:TPU:8, one launch (start us, length us, event | category | flops | bytes accessed | tf_op | source)
XLA Modules:
  0.0 35.8 jit_solution(14902690641797262589)
XLA Ops:
  1.3 32.8 %shard_map.122 = (f32[64]{0:T(128)}, f32[3,64]{1,0:T(4,128)}) custom-call(f32[3,64]{1,0:T(4,128)} %pos_hbm.1, s32[64]{0:T(128)} %spc_hbm.1, bf16[64,128]{1,0:T(8,128)(2,1)} %node_hbm.1, bf16[128,128]{1,0:T(8,128)(2,1)} %wself_hbm.1, bf16[128,128]{1,0:T(8,128)(2,1)} %wsend_hbm.1, f32[8,128]{1,0:T(8,128)} %radial_hbm.1, bf16[128,128]{1,0:T(8,128)(2,1)} %wmix_hbm.1, ...), custom_call_target="tpu_custom_call" | custom-call | tf_op jit(solution)/shard_map/pallas_call
  34.0 0.0 copy-start.1
  34.1 0.0 copy-start
  34.1 0.6 %copy-done.1 = f32[64]{0:T(128)S(1)} copy-done((f32[64]{0:T(128)S(1)}, f32[64]{0:T(128)}, u32[]{:S(2)}) %copy-start.1) | copy-done | bytes 280
  34.7 0.5 %copy.16 = f32[64]{0:T(128)} copy(f32[64]{0:T(128)S(1)} %copy-done.1) | data formatting | bytes 512
  35.2 0.0 copy-done
  35.2 0.6 %copy.17 = f32[3,64]{1,0:T(4,128)} copy(f32[3,64]{1,0:T(4,128)S(1)} %copy-done) | data formatting | bytes 1536
Async XLA Ops:
  34.0 0.6 %copy-start.1 = (f32[64]{0:T(128)S(1)}, f32[64]{0:T(128)}, u32[]{:S(2)}) copy-start(f32[64]{0:T(128)} %get-tuple-element.4) | copy-start | bytes 772
  34.1 1.1 %copy-start = (f32[3,64]{1,0:T(4,128)S(1)}, f32[3,64]{1,0:T(4,128)}, u32[]{:S(2)}) copy-start(f32[3,64]{1,0:T(4,128)} %get-tuple-element.5) | copy-start | bytes 2308
